TPU v7x, 256 devices: a whole 4x4x8 slice. The times are simulated.
256 devices in a mesh: tiles: 256 (over z, x, y, core).
Axes of the slice: x: 4, y: 4, z: 8, core: 2. Of those that a mesh axis runs over, the one named last changes fastest.
Arguments:
- features: bfloat16 [256, 64, 4096], P('tiles'), may hold values from -6 to 6
- weights_first: bfloat16 [9, 64, 64], replicated, may hold values from -0.25 to 0.25
- weights_second: bfloat16 [9, 64, 64], replicated, may hold values from -0.25 to 0.25
- cotangent: bfloat16 [256, 32, 2048], P('tiles'), may hold values from -6 to 6
- neighbours: int32 [256, 8], P('tiles'), may hold values from 0 to 255, as said below
- turns: int32 [256, 8], P('tiles'), may hold values from 0 to 3
- corners: int32 [256, 4], P('tiles'), may hold values 0 or 1
Outputs:
- pooled: bfloat16 [256, 32, 2048], P('tiles')
- grad_features: bfloat16 [256, 64, 4096], P('tiles')
- grad_first: float32 [9, 64, 64], replicated
- grad_second: float32 [9, 64, 64], replicated
Inputs may be any that keep to these rules, and one draw needn't show every extreme that they name: With 1 tiles a device in order, the owner of neighbours[t, j] lies within 3 devices of the owner of t around the cycle of devices, and both 3 devices ahead and behind occur.
All inputs are finite; a program needn't handle non-finite values. No bound on the sum of `corners` on one device may be relied on, other than what follows from the above.
Results may differ from a plain program's by a relative error of at most 0.006.
Values may be sent and summed in bfloat16 or wider, within the bound.
A program may use at most 128 MiB of HBM per device.

v0:
```python
import jax
import jax.numpy as jnp
from jax import lax
from jax.sharding import PartitionSpec as P

REACH = 3


DIRS = ((-1, 0), (-1, 1), (0, 1), (1, 1), (1, 0), (1, -1), (0, -1), (-1, -1))


def from_behind(x, axis, by):
    count = lax.axis_size(axis)
    return lax.ppermute(x, axis, [(i, (i + by) % count) for i in range(count)])


def spans(step, width, tile_side):
    if step < 0:
        return slice(0, width)
    if step == 0:
        return slice(width, width + tile_side)
    return slice(width + tile_side, tile_side + 2 * width)


def needed_edge(dy, dx):
    if dy < 0:
        return 2
    if dy > 0:
        return 0
    if dx < 0:
        return 3
    return 1


def corner_cols(dx, width, tile_side):
    if dx < 0:
        return slice(tile_side - width, tile_side)
    return slice(0, width)


def natural(index, strip):
    if index % 2 == 1:
        return jnp.swapaxes(strip, 0, 1)
    return strip


def edges_of(field, width):
    tile_side = field.shape[1]
    top = field[:, :width]
    left = jnp.swapaxes(field[:, :, :width], 1, 2)
    bottom = field[:, tile_side - width :]
    right = jnp.swapaxes(field[:, :, tile_side - width :], 1, 2)
    return jnp.stack([top, left, bottom, right], 1)


def rim_of(strips, quarter, edge):
    result = None
    for steps in range(4):
        source_tile = (edge - steps) % 4
        candidate = jnp.rot90(natural(source_tile, strips[source_tile]), steps, axes=(0, 1))
        result = candidate if result is None else jnp.where(quarter == steps, candidate, result)
    return result


def extend_tile(owned_tile, nbr_strips, turn_row, corner_row, width):
    tile_side = owned_tile.shape[0]
    blocks = []
    for j, (dy, dx) in enumerate(DIRS):
        rim = rim_of(nbr_strips[j], turn_row[j], needed_edge(dy, dx))
        if dy != 0 and dx != 0:
            rim = rim[:, corner_cols(dx, width, tile_side)] * corner_row[j // 2].astype(rim.dtype)
        blocks.append(rim)
    upper = jnp.concatenate([blocks[7], blocks[0], blocks[1]], 1)
    middle = jnp.concatenate([blocks[6], owned_tile, blocks[2]], 1)
    lower = jnp.concatenate([blocks[5], blocks[4], blocks[3]], 1)
    return jnp.concatenate([upper, middle, lower], 0)


def return_tile(grad_ext, turn_row, corner_row, width):
    tile_side = grad_ext.shape[0] - 2 * width
    chans = grad_ext.shape[2]
    outputs = []
    for j, (dy, dx) in enumerate(DIRS):
        edge = needed_edge(dy, dx)
        block = grad_ext[spans(dy, width, tile_side), spans(dx, width, tile_side)]
        if dy != 0 and dx != 0:
            block = block * corner_row[j // 2].astype(block.dtype)
            placed = (
                jnp.zeros((width, tile_side, chans), block.dtype)
                .at[:, corner_cols(dx, width, tile_side)]
                .set(block)
            )
        else:
            placed = block
        slots = []
        for source_tile in range(4):
            steps = (edge - source_tile) % 4
            back = natural(source_tile, jnp.rot90(placed, -steps, axes=(0, 1)))
            slots.append(jnp.where(turn_row[j] == steps, back, jnp.zeros_like(back)))
        outputs.append(jnp.stack(slots))
    return jnp.stack(outputs)


def convolve_piece(
    source_tile, kernel_weights, dilation_factor, corner_anchor_point, row_total, column_total
):
    running_total = None
    for left_operand in range(3):
        for right_operand in range(3):
            row_start = row_total[0] - corner_anchor_point + left_operand * dilation_factor
            column_start = column_total[0] - corner_anchor_point + right_operand * dilation_factor
            window_patch = source_tile[
                :,
                row_start : row_start + row_total[1] - row_total[0],
                column_start : column_start + column_total[1] - column_total[0],
                :,
            ]
            product_term = jnp.einsum(
                "tijc,cd->tijd",
                window_patch,
                kernel_weights[3 * left_operand + right_operand],
                preferred_element_type=jnp.float32,
            )
            running_total = product_term if running_total is None else running_total + product_term
    return running_total


def transposed_convolve(gradient_tile, kernel_weights, dilation_factor):
    running_total = None
    for left_operand in range(3):
        for right_operand in range(3):
            product_term = jnp.einsum(
                "tijd,cd->tijc",
                gradient_tile,
                kernel_weights[3 * left_operand + right_operand],
                preferred_element_type=jnp.float32,
            )
            product_term = jnp.pad(
                product_term,
                (
                    (0, 0),
                    (left_operand * dilation_factor, (2 - left_operand) * dilation_factor),
                    (right_operand * dilation_factor, (2 - right_operand) * dilation_factor),
                    (0, 0),
                ),
            )
            running_total = product_term if running_total is None else running_total + product_term
    return running_total


def cross_correlate(extended_tile, gradient_tile, dilation_factor):
    tile_side = gradient_tile.shape[1]
    taps = []
    for left_operand in range(3):
        for right_operand in range(3):
            window_patch = extended_tile[
                :,
                left_operand * dilation_factor : left_operand * dilation_factor + tile_side,
                right_operand * dilation_factor : right_operand * dilation_factor + tile_side,
            ]
            taps.append(
                jnp.einsum(
                    "tijc,tijd->cd", window_patch, gradient_tile, preferred_element_type=jnp.float32
                )
            )
    return jnp.stack(taps)


def local(features, weights_first, weights_second, cotangent, neighbours, turns, corners):
    count = features.shape[0]
    tile_side = features.shape[1]
    chans = features.shape[2] // tile_side
    tiles = features.reshape(count, tile_side, tile_side, chans)
    devices = lax.axis_size("tiles")
    here = lax.axis_index("tiles")
    reach = REACH
    delta = (neighbours // count - here + reach) % devices - reach
    slot = (delta + reach) * count + neighbours % count

    def collect(package):
        pieces = {0: package}
        for offset in range(-reach, reach + 1):
            if offset != 0:
                pieces[offset] = from_behind(package, "tiles", -offset)
        return jnp.concatenate([pieces[offset] for offset in range(-reach, reach + 1)], 0)

    def neighbour_extend(owned_tile, width):
        package = edges_of(owned_tile, width).reshape(count, 4 * width, tile_side * chans)
        pool = collect(package).reshape(-1, 4, width, tile_side, chans)
        nbr_strips = pool[slot]
        return jax.vmap(lambda o, n, r, c: extend_tile(o, n, r, c, width))(
            owned_tile, nbr_strips, turns, corners
        )

    def forward_convolve(owned_tile, kernel_weights, dilation_factor):
        extended_tile = neighbour_extend(owned_tile, dilation_factor)
        return (
            extended_tile,
            convolve_piece(
                extended_tile, kernel_weights, dilation_factor, 0, (0, tile_side), (0, tile_side)
            ),
        )

    def give_back(grad_ext, width):
        returned = jax.vmap(lambda g, r, c: return_tile(g, r, c, width))(grad_ext, turns, corners)
        messages = returned.reshape(count * 8, 4 * width * tile_side * chans)
        target = slot.reshape(count * 8)
        places = jnp.arange((2 * reach + 1) * count, dtype=jnp.int32)
        onehot = (target[None, :] == places[:, None]).astype(jnp.float32)
        buffers = jnp.dot(onehot, messages, precision=lax.Precision.HIGHEST)
        buffers = buffers.reshape(2 * reach + 1, count, 4 * width, tile_side * chans)
        running_total = buffers[reach]
        for offset in range(-reach, reach + 1):
            if offset != 0:
                running_total = running_total + from_behind(
                    buffers[offset + reach], "tiles", offset
                )
        strips = running_total.reshape(count, 4, width, tile_side, chans)
        field = grad_ext[:, width : width + tile_side, width : width + tile_side]
        field = field.at[:, :width].add(strips[:, 0])
        field = field.at[:, :, :width].add(jnp.swapaxes(strips[:, 1], 1, 2))
        field = field.at[:, tile_side - width :].add(strips[:, 2])
        field = field.at[:, :, tile_side - width :].add(jnp.swapaxes(strips[:, 3], 1, 2))
        return field

    ext_first, z_first = forward_convolve(tiles, weights_first, 1)
    s_first = jax.nn.sigmoid(z_first)
    y_first = (z_first * s_first).astype(jnp.bfloat16)
    ext_second, z_second = forward_convolve(y_first, weights_second, 2)
    s_second = jax.nn.sigmoid(z_second)
    pooled = (
        (z_second * s_second)
        .reshape(count, tile_side // 2, 2, tile_side // 2, 2, chans)
        .mean(axis=(2, 4))
    )
    pooled = pooled.astype(jnp.bfloat16)
    upstream = cotangent.reshape(count, tile_side // 2, tile_side // 2, chans).astype(jnp.float32)
    g_act = jnp.repeat(jnp.repeat(upstream, 2, 1), 2, 2) * 0.25
    g_second = (g_act * s_second * (1.0 + z_second * (1.0 - s_second))).astype(jnp.bfloat16)
    gext_second = transposed_convolve(g_second, weights_second, 2)
    wgrad_second = cross_correlate(ext_second, g_second, 2)
    g_y_first = give_back(gext_second, 2)
    g_first = (g_y_first * s_first * (1.0 + z_first * (1.0 - s_first))).astype(jnp.bfloat16)
    gext_first = transposed_convolve(g_first, weights_first, 1)
    wgrad_first = cross_correlate(ext_first, g_first, 1)
    g_input = give_back(gext_first, 1)
    grad_first, grad_second = lax.psum((wgrad_first, wgrad_second), "tiles")
    return (
        pooled.reshape(count, tile_side // 2, tile_side // 2 * chans),
        g_input.astype(jnp.bfloat16).reshape(count, tile_side, tile_side * chans),
        grad_first,
        grad_second,
    )


def solution(mesh):
    return jax.shard_map(
        local,
        mesh=mesh,
        in_specs=(
            P("tiles", None, None),
            P(),
            P(),
            P("tiles", None, None),
            P("tiles", None),
            P("tiles", None),
            P("tiles", None),
        ),
        out_specs=(P("tiles", None, None), P("tiles", None, None), P(), P()),
        check_vma=False,
    )
```

profile of v0, /device:TPU:1, one launch (start us, length us, event | category | flops | bytes accessed | tf_op | source)
XLA Modules:
  0.0 545.2 jit_solution(1441004540171688650)
XLA Ops:
  7.3 2.1 reshape.1428
  10.1 11.7 %collective-permute-start.5 = (bf16[1,4,4096]{2,1,0:T(4,128)(2,1)S(1)}, bf16[1,4,4096]{2,1,0:T(4,128)(2,1)S(1)}, u32[]{:S(2)}, u32[]{:S(2)}) collective-permute-start(bf16[1,4,4096]{2,1,0:T(4,128)(2,1)S(1)} %pad_maximum_fusion.21), channel_id=1, source_target_pairs={{0,253},{1,254},{2,255},{3,0},{4,1},{5,2},{6,3},{7,4},{8,5},{9,6},... | collective-permute-start | bytes 98312 | tf_op jit(solution)/shard_map/ppermute | solution.py:14
  56.5 8.2 %collective-permute-done.1 = bf16[1,4,4096]{2,1,0:T(4,128)(2,1)S(1)} collective-permute-done((bf16[1,4,4096]{2,1,0:T(4,128)(2,1)S(1)}, bf16[1,4,4096]{2,1,0:T(4,128)(2,1)S(1)}, u32[]{:S(2)}, u32[]{:S(2)}) %collective-permute-start.1) | collective-permute-done | bytes 32800 | tf_op jit(solution)/shard_map/ppermute | solution.py:14
  69.2 3.0 maximum_maximum_fusion.2
  78.8 3.2 multiply_convert_fusion
  89.6 5.8 %collective-permute-done.6 = bf16[1,8,4096]{2,1,0:T(8,128)(2,1)S(1)} collective-permute-done((bf16[1,8,4096]{2,1,0:T(8,128)(2,1)S(1)}, bf16[1,8,4096]{2,1,0:T(8,128)(2,1)S(1)}, u32[]{:S(2)}, u32[]{:S(2)}) %collective-permute-start.6) | collective-permute-done | bytes 65568 | tf_op jit(solution)/shard_map/ppermute | solution.py:14
  96.3 8.3 %collective-permute-done.7 = bf16[1,8,4096]{2,1,0:T(8,128)(2,1)S(1)} collective-permute-done((bf16[1,8,4096]{2,1,0:T(8,128)(2,1)S(1)}, bf16[1,8,4096]{2,1,0:T(8,128)(2,1)S(1)}, u32[]{:S(2)}, u32[]{:S(2)}) %collective-permute-start.7) | collective-permute-done | bytes 65568 | tf_op jit(solution)/shard_map/ppermute | solution.py:14
  123.6 2.8 maximum_maximum_fusion
  129.9 2.7 fusion.2
  137.5 3.5 pad_add_fusion
  159.5 2.4 fusion.11
  179.2 2.9 stack.428
  182.8 2.6 slice_reduce_fusion.5
  186.4 2.6 fusion.4
  190.5 2.6 copy.1045
  204.4 4.1 reduce_sum.9
  208.5 7.0 %collective-permute-start.12 = (f32[1,8,4096]{2,1,0:T(8,128)}, f32[1,8,4096]{2,1,0:T(8,128)}, u32[]{:S(2)}, u32[]{:S(2)}) collective-permute-start(f32[1,8,4096]{2,1,0:T(8,128)} %squeeze.499), channel_id=1, source_target_pairs={{0,253},{1,254},{2,255},{3,0},{4,1},{5,2},{6,3},{7,4},{8,5},{9,6},... | collective-permute-start | bytes 393224 | tf_op jit(solution)/shard_map/ppermute | solution.py:14
  227.0 3.1 fusion.41
  239.2 3.3 pad_add_fusion.1
  263.4 6.9 %collective-permute-start.19 = (f32[1,4,4096]{2,1,0:T(4,128)S(1)}, f32[1,4,4096]{2,1,0:T(4,128)S(1)}, u32[]{:S(2)}, u32[]{:S(2)}) collective-permute-start(f32[1,4,4096]{2,1,0:T(4,128)S(1)} %squeeze.509), channel_id=1, source_target_pairs={{0,254},{1,255},{2,0},{3,1},{4,2},{5,3},{6,4},{7,5},{8,6},{9,7},{1... | collective-permute-start | bytes 196616 | tf_op jit(solution)/shard_map/ppermute | solution.py:14
  275.3 7.2 %collective-permute-start.18 = (f32[1,4,4096]{2,1,0:T(4,128)S(1)}, f32[1,4,4096]{2,1,0:T(4,128)}, u32[]{:S(2)}, u32[]{:S(2)}) collective-permute-start(f32[1,4,4096]{2,1,0:T(4,128)S(1)} %squeeze.508), channel_id=1, source_target_pairs={{0,253},{1,254},{2,255},{3,0},{4,1},{5,2},{6,3},{7,4},{8,5},{9,6},... | collective-permute-start | bytes 196616 | tf_op jit(solution)/shard_map/ppermute | solution.py:14
  284.4 3.3 slice.1482
  287.8 2.8 copy.1285
  295.6 239.0 %all-reduce.29.cloned.1.call-done = (f32[9,64,64]{2,1,0:T(8,128)}, f32[9,64,64]{2,1,0:T(8,128)}) async-done(((f32[9,64,64]{2,1,0:T(8,128)}, f32[9,64,64]{2,1,0:T(8,128)}), (f32[9,64,64]{2,1,0:T(8,128)}, f32[9,64,64]{2,1,0:T(8,128)})) %all-reduce.29.cloned.1.call-update) | async-done | bytes 294928 | tf_op jit(solution)/shard_map/psum | solution.py:247
  (538 shorter events, 162.6 us)
Async XLA Ops:
  7.2 527.3 %all-reduce.29.cloned.1.call-start = ((), (), s32[]{:S(2)}) async-start(), calls=%async_computation | async-start | bytes 1179648 | tf_op jit(solution)/shard_map/psum | solution.py:247
  10.1 54.8 %collective-permute-start.5 = (bf16[1,4,4096]{2,1,0:T(4,128)(2,1)S(1)}, bf16[1,4,4096]{2,1,0:T(4,128)(2,1)S(1)}, u32[]{:S(2)}, u32[]{:S(2)}) collective-permute-start(bf16[1,4,4096]{2,1,0:T(4,128)(2,1)S(1)} %pad_maximum_fusion.21), channel_id=1, source_target_pairs={{0,253},{1,254},{2,255},{3,0},{4,1},{5,2},{6,3},{7,4},{8,5},{9,6},... | collective-permute-start | bytes 98312 | tf_op jit(solution)/shard_map/ppermute | solution.py:14
  21.8 43.0 %collective-permute-start.4 = (bf16[1,4,4096]{2,1,0:T(4,128)(2,1)S(1)}, bf16[1,4,4096]{2,1,0:T(4,128)(2,1)S(1)}, u32[]{:S(2)}, u32[]{:S(2)}) collective-permute-start(bf16[1,4,4096]{2,1,0:T(4,128)(2,1)S(1)} %pad_maximum_fusion.21), channel_id=1, source_target_pairs={{0,254},{1,255},{2,0},{3,1},{4,2},{5,3},{6,4},{7,5},{8,6},{9,7},{1... | collective-permute-start | bytes 98312 | tf_op jit(solution)/shard_map/ppermute | solution.py:14
  22.2 42.5 %collective-permute-start.3 = (bf16[1,4,4096]{2,1,0:T(4,128)(2,1)S(1)}, bf16[1,4,4096]{2,1,0:T(4,128)(2,1)S(1)}, u32[]{:S(2)}, u32[]{:S(2)}) collective-permute-start(bf16[1,4,4096]{2,1,0:T(4,128)(2,1)S(1)} %pad_maximum_fusion.21), channel_id=1, source_target_pairs={{0,255},{1,0},{2,1},{3,2},{4,3},{5,4},{6,5},{7,6},{8,7},{9,8},{10,... | collective-permute-start | bytes 98312 | tf_op jit(solution)/shard_map/ppermute | solution.py:14
  22.8 41.8 %collective-permute-start.2 = (bf16[1,4,4096]{2,1,0:T(4,128)(2,1)S(1)}, bf16[1,4,4096]{2,1,0:T(4,128)(2,1)S(1)}, u32[]{:S(2)}, u32[]{:S(2)}) collective-permute-start(bf16[1,4,4096]{2,1,0:T(4,128)(2,1)S(1)} %pad_maximum_fusion.21), channel_id=1, source_target_pairs={{0,1},{1,2},{2,3},{3,4},{4,5},{5,6},{6,7},{7,8},{8,9},{9,10},{10,1... | collective-permute-start | bytes 98312 | tf_op jit(solution)/shard_map/ppermute | solution.py:14
  24.0 32.2 %collective-permute-start = (bf16[1,4,4096]{2,1,0:T(4,128)(2,1)S(1)}, bf16[1,4,4096]{2,1,0:T(4,128)(2,1)S(1)}, u32[]{:S(2)}, u32[]{:S(2)}) collective-permute-start(bf16[1,4,4096]{2,1,0:T(4,128)(2,1)S(1)} %pad_maximum_fusion.21), channel_id=1, source_target_pairs={{0,3},{1,4},{2,5},{3,6},{4,7},{5,8},{6,9},{7,10},{8,11},{9,12},{10... | collective-permute-start | bytes 98312 | tf_op jit(solution)/shard_map/ppermute | solution.py:14
  82.3 26.3 %collective-permute-start.11 = (bf16[1,8,4096]{2,1,0:T(8,128)(2,1)S(1)}, bf16[1,8,4096]{2,1,0:T(8,128)(2,1)S(1)}, u32[]{:S(2)}, u32[]{:S(2)}) collective-permute-start(bf16[1,8,4096]{2,1,0:T(8,128)(2,1)S(1)} %reshape.1439), channel_id=1, source_target_pairs={{0,253},{1,254},{2,255},{3,0},{4,1},{5,2},{6,3},{7,4},{8,5},{9,6},... | collective-permute-start | bytes 196616 | tf_op jit(solution)/shard_map/ppermute | solution.py:14
  84.0 23.8 %collective-permute-start.10 = (bf16[1,8,4096]{2,1,0:T(8,128)(2,1)S(1)}, bf16[1,8,4096]{2,1,0:T(8,128)(2,1)S(1)}, u32[]{:S(2)}, u32[]{:S(2)}) collective-permute-start(bf16[1,8,4096]{2,1,0:T(8,128)(2,1)S(1)} %reshape.1439), channel_id=1, source_target_pairs={{0,254},{1,255},{2,0},{3,1},{4,2},{5,3},{6,4},{7,5},{8,6},{9,7},{1... | collective-permute-start | bytes 196616 | tf_op jit(solution)/shard_map/ppermute | solution.py:14
  84.2 22.8 %collective-permute-start.9 = (bf16[1,8,4096]{2,1,0:T(8,128)(2,1)S(1)}, bf16[1,8,4096]{2,1,0:T(8,128)(2,1)S(1)}, u32[]{:S(2)}, u32[]{:S(2)}) collective-permute-start(bf16[1,8,4096]{2,1,0:T(8,128)(2,1)S(1)} %reshape.1439), channel_id=1, source_target_pairs={{0,255},{1,0},{2,1},{3,2},{4,3},{5,4},{6,5},{7,6},{8,7},{9,8},{10,... | collective-permute-start | bytes 196616 | tf_op jit(solution)/shard_map/ppermute | solution.py:14
  84.4 21.0 %collective-permute-start.8 = (bf16[1,8,4096]{2,1,0:T(8,128)(2,1)S(1)}, bf16[1,8,4096]{2,1,0:T(8,128)(2,1)S(1)}, u32[]{:S(2)}, u32[]{:S(2)}) collective-permute-start(bf16[1,8,4096]{2,1,0:T(8,128)(2,1)S(1)} %reshape.1439), channel_id=1, source_target_pairs={{0,1},{1,2},{2,3},{3,4},{4,5},{5,6},{6,7},{7,8},{8,9},{9,10},{10,1... | collective-permute-start | bytes 196616 | tf_op jit(solution)/shard_map/ppermute | solution.py:14
  85.9 9.5 %collective-permute-start.6 = (bf16[1,8,4096]{2,1,0:T(8,128)(2,1)S(1)}, bf16[1,8,4096]{2,1,0:T(8,128)(2,1)S(1)}, u32[]{:S(2)}, u32[]{:S(2)}) collective-permute-start(bf16[1,8,4096]{2,1,0:T(8,128)(2,1)S(1)} %reshape.1439), channel_id=1, source_target_pairs={{0,3},{1,4},{2,5},{3,6},{4,7},{5,8},{6,9},{7,10},{8,11},{9,12},{10... | collective-permute-start | bytes 196616 | tf_op jit(solution)/shard_map/ppermute | solution.py:14
  95.4 9.1 %collective-permute-start.7 = (bf16[1,8,4096]{2,1,0:T(8,128)(2,1)S(1)}, bf16[1,8,4096]{2,1,0:T(8,128)(2,1)S(1)}, u32[]{:S(2)}, u32[]{:S(2)}) collective-permute-start(bf16[1,8,4096]{2,1,0:T(8,128)(2,1)S(1)} %reshape.1439), channel_id=1, source_target_pairs={{0,2},{1,3},{2,4},{3,5},{4,6},{5,7},{6,8},{7,9},{8,10},{9,11},{10,... | collective-permute-start | bytes 196616 | tf_op jit(solution)/shard_map/ppermute | solution.py:14
  186.0 22.5 %collective-permute-start.13 = (f32[1,8,4096]{2,1,0:T(8,128)}, f32[1,8,4096]{2,1,0:T(8,128)}, u32[]{:S(2)}, u32[]{:S(2)}) collective-permute-start(f32[1,8,4096]{2,1,0:T(8,128)} %squeeze.500), channel_id=1, source_target_pairs={{0,254},{1,255},{2,0},{3,1},{4,2},{5,3},{6,4},{7,5},{8,6},{9,7},{1... | collective-permute-start | bytes 393224 | tf_op jit(solution)/shard_map/ppermute | solution.py:14
  201.0 18.8 %collective-permute-start.14 = (f32[1,8,4096]{2,1,0:T(8,128)}, f32[1,8,4096]{2,1,0:T(8,128)}, u32[]{:S(2)}, u32[]{:S(2)}) collective-permute-start(f32[1,8,4096]{2,1,0:T(8,128)} %squeeze.501), channel_id=1, source_target_pairs={{0,255},{1,0},{2,1},{3,2},{4,3},{5,4},{6,5},{7,6},{8,7},{9,8},{10,... | collective-permute-start | bytes 393224 | tf_op jit(solution)/shard_map/ppermute | solution.py:14
  201.5 18.4 %collective-permute-start.15 = (f32[1,8,4096]{2,1,0:T(8,128)}, f32[1,8,4096]{2,1,0:T(8,128)}, u32[]{:S(2)}, u32[]{:S(2)}) collective-permute-start(f32[1,8,4096]{2,1,0:T(8,128)} %squeeze.502), channel_id=1, source_target_pairs={{0,1},{1,2},{2,3},{3,4},{4,5},{5,6},{6,7},{7,8},{8,9},{9,10},{10,1... | collective-permute-start | bytes 393224 | tf_op jit(solution)/shard_map/ppermute | solution.py:14
  202.9 17.0 %collective-permute-start.16 = (f32[1,8,4096]{2,1,0:T(8,128)}, f32[1,8,4096]{2,1,0:T(8,128)}, u32[]{:S(2)}, u32[]{:S(2)}) collective-permute-start(f32[1,8,4096]{2,1,0:T(8,128)} %squeeze.503), channel_id=1, source_target_pairs={{0,2},{1,3},{2,4},{3,5},{4,6},{5,7},{6,8},{7,9},{8,10},{9,11},{10,... | collective-permute-start | bytes 393224 | tf_op jit(solution)/shard_map/ppermute | solution.py:14
  204.0 15.8 %collective-permute-start.17 = (f32[1,8,4096]{2,1,0:T(8,128)}, f32[1,8,4096]{2,1,0:T(8,128)}, u32[]{:S(2)}, u32[]{:S(2)}) collective-permute-start(f32[1,8,4096]{2,1,0:T(8,128)} %squeeze.504), channel_id=1, source_target_pairs={{0,3},{1,4},{2,5},{3,6},{4,7},{5,8},{6,9},{7,10},{8,11},{9,12},{10... | collective-permute-start | bytes 393224 | tf_op jit(solution)/shard_map/ppermute | solution.py:14
  208.5 11.4 %collective-permute-start.12 = (f32[1,8,4096]{2,1,0:T(8,128)}, f32[1,8,4096]{2,1,0:T(8,128)}, u32[]{:S(2)}, u32[]{:S(2)}) collective-permute-start(f32[1,8,4096]{2,1,0:T(8,128)} %squeeze.499), channel_id=1, source_target_pairs={{0,253},{1,254},{2,255},{3,0},{4,1},{5,2},{6,3},{7,4},{8,5},{9,6},... | collective-permute-start | bytes 393224 | tf_op jit(solution)/shard_map/ppermute | solution.py:14
  263.4 11.9 %collective-permute-start.19 = (f32[1,4,4096]{2,1,0:T(4,128)S(1)}, f32[1,4,4096]{2,1,0:T(4,128)S(1)}, u32[]{:S(2)}, u32[]{:S(2)}) collective-permute-start(f32[1,4,4096]{2,1,0:T(4,128)S(1)} %squeeze.509), channel_id=1, source_target_pairs={{0,254},{1,255},{2,0},{3,1},{4,2},{5,3},{6,4},{7,5},{8,6},{9,7},{1... | collective-permute-start | bytes 196616 | tf_op jit(solution)/shard_map/ppermute | solution.py:14
  273.6 17.1 %collective-permute-start.20 = (f32[1,4,4096]{2,1,0:T(4,128)}, f32[1,4,4096]{2,1,0:T(4,128)}, u32[]{:S(2)}, u32[]{:S(2)}) collective-permute-start(f32[1,4,4096]{2,1,0:T(4,128)} %squeeze.510), channel_id=1, source_target_pairs={{0,255},{1,0},{2,1},{3,2},{4,3},{5,4},{6,5},{7,6},{8,7},{9,8},{10,... | collective-permute-start | bytes 196616 | tf_op jit(solution)/shard_map/ppermute | solution.py:14
  274.8 15.9 %collective-permute-start.21 = (f32[1,4,4096]{2,1,0:T(4,128)}, f32[1,4,4096]{2,1,0:T(4,128)}, u32[]{:S(2)}, u32[]{:S(2)}) collective-permute-start(f32[1,4,4096]{2,1,0:T(4,128)} %squeeze.511), channel_id=1, source_target_pairs={{0,1},{1,2},{2,3},{3,4},{4,5},{5,6},{6,7},{7,8},{8,9},{9,10},{10,1... | collective-permute-start | bytes 196616 | tf_op jit(solution)/shard_map/ppermute | solution.py:14
  275.3 15.3 %collective-permute-start.22 = (f32[1,4,4096]{2,1,0:T(4,128)S(1)}, f32[1,4,4096]{2,1,0:T(4,128)}, u32[]{:S(2)}, u32[]{:S(2)}) collective-permute-start(f32[1,4,4096]{2,1,0:T(4,128)S(1)} %squeeze.512), channel_id=1, source_target_pairs={{0,2},{1,3},{2,4},{3,5},{4,6},{5,7},{6,8},{7,9},{8,10},{9,11},{10,... | collective-permute-start | bytes 196616 | tf_op jit(solution)/shard_map/ppermute | solution.py:14
  275.3 15.3 %collective-permute-start.23 = (f32[1,4,4096]{2,1,0:T(4,128)S(1)}, f32[1,4,4096]{2,1,0:T(4,128)}, u32[]{:S(2)}, u32[]{:S(2)}) collective-permute-start(f32[1,4,4096]{2,1,0:T(4,128)S(1)} %squeeze.513), channel_id=1, source_target_pairs={{0,3},{1,4},{2,5},{3,6},{4,7},{5,8},{6,9},{7,10},{8,11},{9,12},{10... | collective-permute-start | bytes 196616 | tf_op jit(solution)/shard_map/ppermute | solution.py:14
  275.3 15.3 %collective-permute-start.18 = (f32[1,4,4096]{2,1,0:T(4,128)S(1)}, f32[1,4,4096]{2,1,0:T(4,128)}, u32[]{:S(2)}, u32[]{:S(2)}) collective-permute-start(f32[1,4,4096]{2,1,0:T(4,128)S(1)} %squeeze.508), channel_id=1, source_target_pairs={{0,253},{1,254},{2,255},{3,0},{4,1},{5,2},{6,3},{7,4},{8,5},{9,6},... | collective-permute-start | bytes 196616 | tf_op jit(solution)/shard_map/ppermute | solution.py:14
  (76 other events, 362.0 us)
Sparse Core Ops, SparseCore 0:
  290.7 243.7 all-reduce.28
where the time goes:
time: 554 us; the launch traced here: 545 us
  waiting for transfers between devices  261 us (47%)
  local copies, waits for them, and re-layouts  86.5 us (16%)
  matrix products  59.2 us (11%)
  other arithmetic  49 us (9%)
  starting transfers between devices  47.5 us (9%)
  between operations  41.7 us (8%)
    psum x1, waiting for transfers between devices, local(): grad_first, grad_second = lax.psum((wgrad_first, wgrad_second), 'tiles')  239 us
    ppermute x24, starting transfers between devices, from_behind(): return lax.ppermute(x, axis, [(i, (i + by) % count) for i in range(count)])  47.5 us
    dot_general x18, matrix products, cross_correlate(): jnp.einsum('tijc,tijd->cd', window_patch, gradient_tile, preferred_elemen...  29.2 us
    ppermute x24, waiting for transfers between devices, from_behind(): return lax.ppermute(x, axis, [(i, (i + by) % count) for i in range(count)])  22.3 us
    unnamed x167, local copies, waits for them, and re-layouts  19.1 us
    dot_general x18, matrix products, convolve_piece(): jnp.einsum('tijc,cd->tijd', window_patch, kernel_weights[3 * left_operand...  18.2 us
    another operation x57, other arithmetic, return_tile(): outputs.append(jnp.stack(slots))  12 us
  transfers between devices with their start and end apart: 25, of which 4 were waited for; matrix products, arithmetic and copies ran while one was open for 9% of the time, Pallas kernels for 0%

commit v1 on v0

v1 whole, which is shorter than its diff:
```python
import functools

import jax
import jax.numpy as jnp
from jax import lax
from jax.experimental import pallas as pl
from jax.experimental.pallas import tpu as pltpu
from jax.sharding import PartitionSpec as P

REACH = 3
SLOTS = 2 * REACH + 1
SIDE = 64
CHANS = 64
PAIRS = SIDE // 2
ROWS = PAIRS * SIDE
STRIP = 4 * SIDE
GROUP = 16
SHARE = 24
CHUNK = 8
RIMS = 4 * SIDE + 32
MESH = pl.DeviceIdType.MESH
BF16 = jnp.bfloat16
F32 = jnp.float32
EDGE_DIRS = ((0, 2), (2, 1), (4, 0), (6, 3))
CORNER_DIRS = ((1, 2, False), (3, 0, False), (5, 0, True), (7, 2, True))
OFFSETS = (1, -1, 2, -2, 3, -3)


def dot(a, b):
    return jnp.dot(a, b, preferred_element_type=F32)


def dot_rows(a, b):
    return lax.dot_general(a, b, (((0,), (0,)), ((), ())), preferred_element_type=F32)


def half_turn(x):
    return pltpu.roll(x, 64, axis=1)


def low_half(x):
    return lax.broadcasted_iota(jnp.int32, x.shape, 1) < 64


def swap(x, y):
    low = low_half(x)
    return jnp.where(low, x, half_turn(y)), jnp.where(low, half_turn(x), y)


def sigmoid(z):
    return 1.0 / (1.0 + jnp.exp(-z))


def plane_peer(here, member):
    return here // 32 * 32 + member * 2 + here % 2


def column_peer(here, member):
    return member // 2 * 32 + here // 2 % 16 * 2 + member % 2


def blocks_of(w_ref, dilation, turned):
    taps = [w_ref[t].astype(F32) for t in range(9)]
    if turned:
        taps = [jnp.transpose(tap) for tap in taps]
    zero = jnp.zeros((CHANS, CHANS), F32)
    result = {}
    for a in range(3):
        left, mid, right = taps[3 * a : 3 * a + 3]
        if dilation == 2:
            quads = {d: (w, zero, zero, w) for d, w in ((-1, left), (0, mid), (1, right))}
        else:
            quads = {-1: (zero, zero, left, zero), 0: (mid, left, right, mid), 1: (zero, right, zero, zero)}
        for d, (q00, q01, q10, q11) in quads.items():
            if turned:
                q01, q10 = q10, q01
                d = -d
            block = jnp.concatenate(
                [jnp.concatenate([q00, q01], 1), jnp.concatenate([q10, q11], 1)], 0
            )
            result[a, d] = block.astype(BF16)
    return result


def fill_weights(w_ref, dilation, turned, big):
    for (a, d), block in blocks_of(w_ref, dilation, turned).items():
        big[(d + 1) * 128 : (d + 2) * 128, a * 128 : (a + 1) * 128] = block


def combine(product, dilation, turned):
    rows = product.shape[0]
    up, mid, down = product[:, :128], product[:, 128:256], product[:, 256:]
    if turned:
        up, down = down, up
    i = lax.broadcasted_iota(jnp.int32, (rows, 128), 0) % SIDE
    up = jnp.where(i >= dilation, pltpu.roll(up, dilation, axis=0), 0.0)
    down = jnp.where(i < SIDE - dilation, pltpu.roll(down, rows - dilation, axis=0), 0.0)
    return mid + up + down


def neighbouring(x_ref, start, count):
    parts = [x_ref[pl.ds(start + k, count)].reshape(count * SIDE, 128) for k in range(3)]
    return jnp.concatenate(parts, 1)


def chunks(body):
    def step(c, unused):
        body(c)
        return unused

    lax.fori_loop(0, PAIRS // CHUNK, step, 0)


def chunk_rows(c):
    return pl.ds(pl.multiple_of(c * (CHUNK * SIDE), CHUNK * SIDE), CHUNK * SIDE)


def convolve(x_ref, big, z_ref, dilation):
    def body(c):
        product = dot(neighbouring(x_ref, c * CHUNK, CHUNK), big[...])
        z_ref[chunk_rows(c), :] = combine(product, dilation, False)

    chunks(body)


def keep_edges(edge_ref, c, value):
    value = value.reshape(CHUNK, SIDE, 128)
    place = pl.ds(pl.multiple_of(c * (CHUNK * 8), CHUNK * 8), CHUNK * 8)
    edge_ref[0, place, :] = value[:, :8].reshape(CHUNK * 8, 128)
    edge_ref[1, place, :] = value[:, SIDE - 8 :].reshape(CHUNK * 8, 128)


def edge_row(edge_ref, side, depth):
    return edge_ref[side, pl.ds(depth if side == 0 else 7 - depth, PAIRS, stride=8), :]


def write_strips(x_ref, edge_ref, strip_ref):
    top = swap(edge_row(edge_ref, 0, 0), edge_row(edge_ref, 0, 1))
    bottom = swap(edge_row(edge_ref, 1, 0), edge_row(edge_ref, 1, 1))
    strip_ref[0:64] = jnp.concatenate(top, 0).astype(BF16)
    strip_ref[64:128] = x_ref[1]
    strip_ref[128:192] = jnp.concatenate(bottom, 0).astype(BF16)
    strip_ref[192:256] = half_turn(x_ref[PAIRS].astype(F32)).astype(BF16)


def fill_select(here, devices, nbr_ref, turn_ref, corner_ref, select):
    def slot_of(j):
        return lax.rem(nbr_ref[0, j] - here + REACH + devices, devices)

    def columns_of(p, edge, quarter, flips):
        source = lax.rem(edge + 4 - quarter, 4)
        flip = jnp.where(quarter == flips[0], 1, jnp.where(quarter == flips[1], 1, 0))
        p = p + flip * (63 - 2 * p)
        split = (p % 2) * 32 + p // 2
        place = split + lax.rem(source, 2) * (p - split)
        return source * 64 + place

    lane = lax.broadcasted_iota(jnp.int32, (SIDE, STRIP), 1)
    row = lax.broadcasted_iota(jnp.int32, (SIDE, STRIP), 0)
    for n, (j, edge) in enumerate(EDGE_DIRS):
        if edge % 2 == 0:
            cols = columns_of(row % 32 * 2 + row // 32, edge, turn_ref[0, j], (2, 3))
        else:
            cols = columns_of(row, edge, turn_ref[0, j], (1, 2))
        hit = jnp.where(lane == cols, 1.0, 0.0)
        slot = slot_of(j)
        for k in range(SLOTS):
            select[k, n * 64 : (n + 1) * 64] = (hit * jnp.where(slot == k, 1.0, 0.0)).astype(BF16)
    lane = lane[:8]
    row = row[:8]
    hits = []
    for j, edge, last in CORNER_DIRS:
        cols = columns_of(63 - row if last else row, edge, turn_ref[0, j], (2, 3))
        hit = jnp.where(lane == cols, 1.0, 0.0) * jnp.where(row < 2, 1.0, 0.0)
        hits.append((hit * corner_ref[0, j // 2].astype(F32), slot_of(j)))
    for k in range(SLOTS):
        parts = [hit * jnp.where(slot == k, 1.0, 0.0) for hit, slot in hits]
        select[k, 256:288] = jnp.concatenate(parts, 0).astype(BF16)


def place_rims(rims, x_ref, rows_ref):
    north, east, south, west = (rims[64 * n : 64 * n + 64] for n in range(4))
    x_ref[PAIRS + 1] = east.astype(BF16)
    x_ref[0] = half_turn(west).astype(BF16)
    ne, se, sw, nw = (rims[256 + 8 * n : 264 + 8 * n] for n in range(4))
    for base, strip, right, left in ((0, north, ne, nw), (2, south, se, sw)):
        inner = swap(strip[:32], strip[32:])
        ends = swap(right[0:1], right[1:2])
        starts = swap(left[1:2], left[0:1])
        for d in range(2):
            rows_ref[base + d, 8:40, :] = inner[d]
            rows_ref[base + d, 40:41, :] = ends[d]
            rows_ref[base + d, 7:8, :] = starts[d]


def strips_beside(rows_ref):
    parts = []
    for k in range(4):
        parts.append(jnp.concatenate([rows_ref[k, 7 + d : 39 + d, :] for d in range(3)], 1))
    return jnp.concatenate(parts, 0).astype(BF16)


def add_rims(x_ref, beside, big, z_ref, dilation):
    west = combine(dot(x_ref[0], big[0:128, :]), dilation, False)
    z_ref[0:64, :] += west
    east = combine(dot(x_ref[PAIRS + 1], big[256:384, :]), dilation, False)
    z_ref[ROWS - 64 : ROWS, :] += east
    north = dot(beside[:64], big[:, 0:128])
    south = dot(beside[64:], big[:, 256:384])
    for d in range(dilation):
        z_ref[pl.ds(dilation - 1 - d, PAIRS, stride=SIDE), :] += north[32 * d : 32 * d + 32]
        z_ref[pl.ds(SIDE - dilation + d, PAIRS, stride=SIDE), :] += south[32 * d : 32 * d + 32]


def transposed(g_ref, big, z_ref, edge_ref, dilation):
    def keep(place, product):
        count = product.shape[0] // SIDE
        value = product.reshape(count, SIDE, 384)
        edge_ref[0, place, :] = value[:, :8, 0:128].reshape(count * 8, 128)
        edge_ref[1, place, :] = value[:, SIDE - 8 :, 256:384].reshape(count * 8, 128)

    def body(c):
        product = dot(neighbouring(g_ref, c * CHUNK, CHUNK), big[...])
        z_ref[chunk_rows(c), :] = combine(product, dilation, True)
        keep(pl.ds(pl.multiple_of(c * (CHUNK * 8) + 8, 8), CHUNK * 8), product)

    chunks(body)
    before = dot(g_ref[1], big[256:384, :])
    after = dot(g_ref[PAIRS], big[0:128, :])
    keep(pl.ds(0, 8), before)
    keep(pl.ds(8 * PAIRS + 8, 8), after)
    return combine(before, dilation, True), combine(after, dilation, True)


def leaving_rims(edge_ref, before, after, dilation):
    def row_strip(side, depth, start, count):
        if depth >= dilation:
            return jnp.zeros((count, 128), F32)
        row = dilation - 1 - depth if side == 0 else 8 - dilation + depth
        if count == 1:
            return edge_ref[side, 8 * start + row : 8 * start + row + 1, :]
        return edge_ref[side, pl.ds(8 * start + row, count, stride=8), :]

    strips, corners = [], []
    gap = jnp.zeros((6, 128), F32)
    for side in range(2):
        inner = [row_strip(side, d, 1, PAIRS) for d in range(2)]
        strips.append(jnp.concatenate(swap(*inner), 0))
        first, second = swap(*[row_strip(side, d, PAIRS + 1, 1) for d in range(2)])
        right = jnp.concatenate([first, second, gap], 0)
        second, first = swap(*[row_strip(side, d, 0, 1) for d in range(2)])
        left = jnp.concatenate([first, second, gap], 0)
        corners.append((right, left))
    order = [strips[0], after, strips[1], half_turn(before)]
    order += [corners[0][0], corners[1][0], corners[1][1], corners[0][1]]
    return jnp.concatenate(order, 0).astype(BF16)


def add_returned(strips, z_ref, dilation):
    z_ref[0:64, :] += strips[64:128]
    z_ref[ROWS - 64 : ROWS, :] += half_turn(strips[192:256])
    top = swap(strips[0:32], strips[32:64])
    bottom = swap(strips[128:160], strips[160:192])
    for d in range(dilation):
        z_ref[pl.ds(d, PAIRS, stride=SIDE), :] += top[d]
        z_ref[pl.ds(SIDE - 1 - d, PAIRS, stride=SIDE), :] += bottom[d]


def write_gradient(c, g, dilation, g_ref, shifted, edge_ref):
    rows = CHUNK * SIDE
    g_ref[pl.ds(c * CHUNK + 1, CHUNK)] = g.astype(BF16).reshape(CHUNK, SIDE, 128)
    i = lax.broadcasted_iota(jnp.int32, (rows, 128), 0) % SIDE
    up = jnp.where(i < SIDE - dilation, pltpu.roll(g, rows - dilation, axis=0), 0.0)
    down = jnp.where(i >= dilation, pltpu.roll(g, dilation, axis=0), 0.0)
    shifted[chunk_rows(c), 0:128] = up.astype(BF16)
    shifted[chunk_rows(c), 128:256] = g.astype(BF16)
    shifted[chunk_rows(c), 256:384] = down.astype(BF16)
    keep_edges(edge_ref, c, g)


def weight_gradient(x_ref, shifted, beside, edge_ref, raw, dilation):
    strip_grads = []
    zero = jnp.zeros((PAIRS, 128), F32)
    for side in range(2):
        for d in range(2):
            if d >= dilation:
                part = jnp.zeros((PAIRS, 384), F32)
            else:
                row = edge_row(edge_ref, side, dilation - 1 - d)
                part = jnp.concatenate([row, zero, zero] if side == 0 else [zero, zero, row], 1)
            strip_grads.append(part)
    strip_grads = jnp.concatenate(strip_grads, 0).astype(BF16)
    for k in range(3):
        total = dot_rows(x_ref[k : k + PAIRS].reshape(ROWS, 128), shifted[...])
        raw[k] = total + dot_rows(beside[:, 128 * k : 128 * k + 128], strip_grads)
    taps = []
    for a in range(3):
        lanes = slice(128 * a, 128 * a + 128)
        upper = [raw[k, 0:64, lanes] for k in range(3)]
        lower = [raw[k, 64:128, lanes] for k in range(3)]
        if dilation == 2:
            taps += [upper[k] + half_turn(lower[k]) for k in range(3)]
        else:
            taps.append(half_turn(upper[1]) + lower[0])
            taps.append(upper[1] + half_turn(lower[1]))
            taps.append(lower[1] + half_turn(upper[2]))
    zero = jnp.zeros((CHANS, 128), F32)
    taps.append(zero)
    low = low_half(zero)
    packed = [jnp.where(low, taps[t], half_turn(taps[t + 1])) for t in range(0, 10, 2)] + [zero]
    return jnp.concatenate(packed, 0).reshape(GROUP, SHARE, 128)


def write_taps(total_ref, out_ref):
    flat = total_ref[...].reshape(GROUP * SHARE, 128)
    for t in range(9):
        block = flat[t // 2 * 64 : t // 2 * 64 + 64]
        if t % 2 == 1:
            block = half_turn(block)
        out_ref[t] = block[:, :CHANS]


class Ring:
    def __init__(self, here, devices, source, target, send, recv):
        self.here, self.devices = here, devices
        self.source, self.target, self.send, self.recv = source, target, send, recv

    def copy(self, offset):
        return pltpu.make_async_remote_copy(
            src_ref=self.source(offset),
            dst_ref=self.target.at[REACH - offset],
            send_sem=self.send.at[REACH + offset],
            recv_sem=self.recv.at[REACH - offset],
            device_id=(lax.rem(self.here + offset + self.devices, self.devices),),
            device_id_type=MESH,
        )

    def start(self, offset):
        self.copy(offset).start()

    def arrived(self, slot):
        there = self.target.at[slot]
        pltpu.make_async_copy(there, there, self.recv.at[slot]).wait()

    def finish(self):
        for offset in OFFSETS:
            self.copy(offset).wait_send()


class Reduction:
    def __init__(self, here, src, plane, column, out, sems):
        self.here, self.src, self.plane, self.column, self.out = here, src, plane, column, out
        self.sems = sems
        self.me = here // 2 % 16
        self.level = here // 32 * 2 + here % 2

    def scatter_copy(self, k):
        peer = (self.me + k) % GROUP
        return pltpu.make_async_remote_copy(
            src_ref=self.src.at[peer], dst_ref=self.plane.at[self.me],
            send_sem=self.sems.at[0, peer], recv_sem=self.sems.at[1, self.me],
            device_id=(plane_peer(self.here, peer),), device_id_type=MESH,
        )

    def column_copy(self, k):
        peer = (self.level + k) % GROUP
        return pltpu.make_async_remote_copy(
            src_ref=self.column.at[self.level], dst_ref=self.column.at[self.level],
            send_sem=self.sems.at[2, peer], recv_sem=self.sems.at[3, self.level],
            device_id=(column_peer(self.here, peer),), device_id_type=MESH,
        )

    def gather_copy(self, k):
        peer = (self.me + k) % GROUP
        return pltpu.make_async_remote_copy(
            src_ref=self.out.at[self.me], dst_ref=self.out.at[self.me],
            send_sem=self.sems.at[4, peer], recv_sem=self.sems.at[5, self.me],
            device_id=(plane_peer(self.here, peer),), device_id_type=MESH,
        )

    def each(self, act):
        def body(k, unused):
            act(k)
            return unused

        lax.fori_loop(1, GROUP, body, 0)

    def arrivals(self, buffer, row, mine):
        def one(k):
            there = buffer.at[(mine + k) % GROUP]
            pltpu.make_async_copy(there, there, self.sems.at[row, (mine + k) % GROUP]).wait()

        self.each(one)

    def scatter(self, value):
        self.src[...] = value
        self.each(lambda k: self.scatter_copy(k).start())
        self.plane[self.me] = self.src[self.me]

    def across(self):
        self.arrivals(self.plane, 1, self.me)
        self.column[self.level] = jnp.sum(self.plane[...], axis=0)
        self.each(lambda k: self.column_copy(k).start())

    def gather(self):
        self.arrivals(self.column, 3, self.level)
        self.out[self.me] = jnp.sum(self.column[...], axis=0)
        self.each(lambda k: self.gather_copy(k).start())

    def finish(self):
        self.arrivals(self.out, 5, self.me)
        self.each(lambda k: self.scatter_copy(k).wait_send())
        self.each(lambda k: self.column_copy(k).wait_send())
        self.each(lambda k: self.gather_copy(k).wait_send())


def level_kernel(
    devices,
    f_ref, w1_ref, w2_ref, cot_ref, nbr_ref, turn_ref, corner_ref,
    pooled_ref, gin_ref, dw1_ref, dw2_ref,
    x1, x2, g_ref, shifted, z_ref, d_ref, act_ref, edge_ref, wide_edge, rows1, rows2, raw,
    big1, big1t, big2, big2t, select,
    pool1, pool2, out2, back2, out1, back1,
    src2, plane2, column2, total2, src1, plane1, column1, total1,
    ring_sems, sems2, sems1,
):
    here = lax.axis_index("tiles")
    barrier = pltpu.get_barrier_semaphore()

    def greet(device):
        pl.semaphore_signal(barrier, inc=1, device_id=(device,), device_id_type=MESH)

    for offset in OFFSETS:
        greet(lax.rem(here + offset + devices, devices))

    def greet_group(k, unused):
        greet(plane_peer(here, (here // 2 + k) % GROUP))
        greet(column_peer(here, (here // 32 * 2 + here % 2 + k) % GROUP))
        return unused

    lax.fori_loop(1, GROUP, greet_group, 0)

    for jp in range(PAIRS):
        x1[jp + 1] = f_ref[:, 128 * jp : 128 * jp + 128]
    empty = jnp.zeros((SIDE, 128), BF16)
    for x in (x1, x2, g_ref):
        x[0] = empty
        x[PAIRS + 1] = empty
    for jp in range(PAIRS):
        edge_ref[0, 8 * jp : 8 * jp + 8, :] = f_ref[0:16, 128 * jp : 128 * jp + 128].astype(F32)[:8]
        edge_ref[1, 8 * jp : 8 * jp + 8, :] = f_ref[48:64, 128 * jp : 128 * jp + 128].astype(F32)[8:]
    write_strips(x1, edge_ref, pool1.at[REACH])

    ring1 = Ring(here, devices, lambda o: pool1.at[REACH], pool1, ring_sems.at[0], ring_sems.at[1])
    ring2 = Ring(here, devices, lambda o: pool2.at[REACH], pool2, ring_sems.at[2], ring_sems.at[3])
    ring3 = Ring(here, devices, lambda o: out2.at[REACH + o], back2, ring_sems.at[4], ring_sems.at[5])
    ring4 = Ring(here, devices, lambda o: out1.at[REACH + o], back1, ring_sems.at[6], ring_sems.at[7])
    sum2 = Reduction(here, src2, plane2, column2, total2, sems2)
    sum1 = Reduction(here, src1, plane1, column1, total1, sems1)

    def collect(ring, pool):
        rims = dot(select[REACH], pool[REACH])
        for offset in OFFSETS:
            slot = REACH - offset
            ring.arrived(slot)
            rims = rims + dot(select[slot], pool[slot])
        return rims

    def send_back(ring, out_ref, rims):
        for offset in OFFSETS:
            out_ref[REACH + offset] = dot_rows(select[REACH + offset], rims).astype(BF16)
            ring.start(offset)
        return dot_rows(select[REACH], rims)

    def take_back(ring, back_ref, own):
        for offset in OFFSETS:
            ring.arrived(REACH - offset)
            own = own + back_ref[REACH - offset].astype(F32)
        return own

    pl.semaphore_wait(barrier, 2 * REACH + 2 * (GROUP - 1))
    for offset in OFFSETS:
        ring1.start(offset)

    fill_weights(w1_ref, 1, False, big1)
    convolve(x1, big1, z_ref, 1)
    fill_select(here, devices, nbr_ref, turn_ref, corner_ref, select)
    fill_weights(w2_ref, 2, False, big2)
    fill_weights(w2_ref, 2, True, big2t)
    fill_weights(w1_ref, 1, True, big1t)
    low = lax.broadcasted_iota(jnp.int32, (PAIRS, 128), 1) < 64
    for t in range(PAIRS // 2):
        both = cot_ref[:, 128 * t : 128 * t + 128].astype(F32) * 0.25
        turned = half_turn(both)
        for jp, value in ((2 * t, jnp.where(low, both, turned)), (2 * t + 1, jnp.where(low, turned, both))):
            act_ref[pl.ds(SIDE * jp, PAIRS, stride=2), :] = value
            act_ref[pl.ds(SIDE * jp + 1, PAIRS, stride=2), :] = value
    place_rims(collect(ring1, pool1), x1, rows1)
    beside1 = strips_beside(rows1)
    add_rims(x1, beside1, big1, z_ref, 1)

    def activate(c):
        z = z_ref[chunk_rows(c), :]
        s = sigmoid(z)
        y = z * s
        d_ref[chunk_rows(c), :] = s * (1.0 + z * (1.0 - s))
        x2[pl.ds(c * CHUNK + 1, CHUNK)] = y.astype(BF16).reshape(CHUNK, SIDE, 128)
        keep_edges(edge_ref, c, y)

    chunks(activate)
    write_strips(x2, edge_ref, pool2.at[REACH])
    for offset in OFFSETS:
        ring2.start(offset)

    convolve(x2, big2, z_ref, 2)
    place_rims(collect(ring2, pool2), x2, rows2)
    beside2 = strips_beside(rows2)
    add_rims(x2, beside2, big2, z_ref, 2)

    def second(c):
        z = z_ref[chunk_rows(c), :]
        s = sigmoid(z)
        z_ref[chunk_rows(c), :] = z * s * 0.25
        g = act_ref[chunk_rows(c), :] * s * (1.0 + z * (1.0 - s))
        write_gradient(c, g.astype(BF16).astype(F32), 2, g_ref, shifted, edge_ref)

    chunks(second)
    for t in range(PAIRS // 2):
        sums = []
        for jp in (2 * t, 2 * t + 1):
            v = z_ref[pl.ds(SIDE * jp, PAIRS, stride=2), :] + z_ref[pl.ds(SIDE * jp + 1, PAIRS, stride=2), :]
            sums.append(v + half_turn(v))
        pooled_ref[:, 128 * t : 128 * t + 128] = jnp.where(low, sums[0], sums[1]).astype(BF16)

    before, after = transposed(g_ref, big2t, z_ref, wide_edge, 2)
    own = send_back(ring3, out2, leaving_rims(wide_edge, before, after, 2))
    sum2.scatter(weight_gradient(x2, shifted, beside2, edge_ref, raw, 2))
    add_returned(take_back(ring3, back2, own), z_ref, 2)

    def first(c):
        g = z_ref[chunk_rows(c), :] * d_ref[chunk_rows(c), :]
        write_gradient(c, g.astype(BF16).astype(F32), 1, g_ref, shifted, edge_ref)

    chunks(first)
    sum2.across()

    sum1.scatter(weight_gradient(x1, shifted, beside1, edge_ref, raw, 1))
    before, after = transposed(g_ref, big1t, z_ref, wide_edge, 1)
    own = send_back(ring4, out1, leaving_rims(wide_edge, before, after, 1))
    sum2.gather()
    sum1.across()
    add_returned(take_back(ring4, back1, own), z_ref, 1)
    for jp in range(PAIRS):
        gin_ref[:, 128 * jp : 128 * jp + 128] = z_ref[SIDE * jp : SIDE * jp + SIDE, :].astype(BF16)
    sum1.gather()
    sum2.finish()
    write_taps(total2, dw2_ref)
    for ring in (ring1, ring2, ring3, ring4):
        ring.finish()
    sum1.finish()
    write_taps(total1, dw1_ref)


def local(features, weights_first, weights_second, cotangent, neighbours, turns, corners):
    devices = lax.axis_size("tiles")
    vmem = pl.BlockSpec(memory_space=pltpu.VMEM)
    smem = pl.BlockSpec(memory_space=pltpu.SMEM)
    slabs = pltpu.VMEM((PAIRS + 2, SIDE, 128), BF16)
    field = pltpu.VMEM((ROWS, 128), F32)
    big = pltpu.VMEM((384, 384), BF16)
    pool = pltpu.VMEM((SLOTS, STRIP, 128), BF16)
    share = pltpu.VMEM((GROUP, SHARE, 128), F32)
    pooled, grad, first, second = pl.pallas_call(
        functools.partial(level_kernel, devices),
        out_shape=(
            jax.ShapeDtypeStruct((PAIRS, PAIRS * CHANS), BF16),
            jax.ShapeDtypeStruct((SIDE, SIDE * CHANS), BF16),
            jax.ShapeDtypeStruct((9, CHANS, CHANS), F32),
            jax.ShapeDtypeStruct((9, CHANS, CHANS), F32),
        ),
        in_specs=[vmem] * 4 + [smem] * 3,
        out_specs=[vmem] * 4,
        scratch_shapes=[
            slabs, slabs, slabs,
            pltpu.VMEM((ROWS, 384), BF16),
            field, field, field,
            pltpu.VMEM((2, 8 * PAIRS, 128), F32),
            pltpu.VMEM((2, 8 * PAIRS + 16, 128), F32),
            pltpu.VMEM((4, 48, 128), F32),
            pltpu.VMEM((4, 48, 128), F32),
            pltpu.VMEM((3, 128, 384), F32),
            big, big, big, big,
            pltpu.VMEM((SLOTS, RIMS, STRIP), BF16),
            pool, pool, pool, pool, pool, pool,
            share, share, share, share, share, share, share, share,
            pltpu.SemaphoreType.DMA((8, SLOTS)),
            pltpu.SemaphoreType.DMA((6, GROUP)),
            pltpu.SemaphoreType.DMA((6, GROUP)),
        ],
        compiler_params=pltpu.CompilerParams(
            collective_id=0, has_side_effects=True, vmem_limit_bytes=48 * 2**20
        ),
        name="level",
    )(features[0], weights_first, weights_second, cotangent[0], neighbours, turns, corners)
    return pooled[None], grad[None], first, second


def solution(mesh):
    return jax.shard_map(
        local,
        mesh=mesh,
        in_specs=(
            P("tiles", None, None),
            P(),
            P(),
            P("tiles", None, None),
            P("tiles", None),
            P("tiles", None),
            P("tiles", None),
        ),
        out_specs=(P("tiles", None, None), P("tiles", None, None), P(), P()),
        check_vma=False,
    )
```

time: 554 us -> 74.2 us (0.13); the launches traced: 545 us -> 74 us
  waiting for transfers between devices: 261 us -> 0 us
  local copies, waits for them, and re-layouts: 86.5 us -> 7.3 us
  Pallas kernels: 0 us -> 66 us
  matrix products: 59.2 us -> 0 us
  other arithmetic: 49 us -> 0 us
  starting transfers between devices: 47.5 us -> 0 us
  between operations: 41.7 us -> 0.67 us
    psum x1 -> x0, waiting for transfers between devices: 239 us -> none  [local(): grad_first, grad_second = lax.psum((wgrad_first, wgrad_second), 'tiles')]
    pallas_call x0 -> x1, Pallas kernels: none -> 66 us  [local(): pl.pallas_call(functools.partial(level_kernel, devices), out_shape=(jax.S...]
    dot_general x56 -> x0, matrix products: 59.2 us -> none  [the longest x18 29.2 us: cross_correlate(): jnp.einsum('tijc,tijd->cd', window_patch, gradient_tile, preferred_elemen...]
    ppermute x24 -> x0, starting transfers between devices: 47.5 us -> none  [from_behind(): return lax.ppermute(x, axis, [(i, (i + by) % count) for i in range(count)])]
    ppermute x24 -> x0, waiting for transfers between devices: 22.3 us -> none  [from_behind(): return lax.ppermute(x, axis, [(i, (i + by) % count) for i in range(count)])]
    another operation x61 -> x0, other arithmetic: 16.2 us -> none  [the longest x57 12 us: return_tile(): outputs.append(jnp.stack(slots))]
    another operation x48 -> x0, local copies, waits for them, and re-layouts: 13.8 us -> none  [the longest x18 10.7 us: return_tile(): return jnp.stack(outputs)]
    squeeze x22 -> x0, local copies, waits for them, and re-layouts: 13.3 us -> none  [the longest x12 10 us: give_back(): buffers[offset + reach]]
  transfers between devices with their start and end apart: 25 -> 0, of which waited for: 4 -> 0; matrix products, arithmetic and copies ran while one was open for 9% -> 0% of each run, Pallas kernels for 0% -> 0%
where the time goes in v1:
time: 74.2 us; the launch traced here: 74 us
  Pallas kernels  66 us (89%)
  local copies, waits for them, and re-layouts  7.3 us (10%)
    pallas_call x1, Pallas kernels, local(): pl.pallas_call(functools.partial(level_kernel, devices), out_shape=(jax.S...  66 us
    unnamed x18, local copies, waits for them, and re-layouts  7.3 us

profile of v1, /device:TPU:1, one launch (start us, length us, event | category | flops | bytes accessed | tf_op | source)
XLA Modules:
  0.0 74.0 jit_solution(7731365442254024348)
XLA Ops:
  0.6 0.0 copy-start.4
  0.6 0.0 copy-start.5
  0.7 0.0 copy-start.6
  0.7 0.6 copy-done.4
  1.3 0.0 copy-done.5
  1.3 0.0 copy-done.6
  1.3 0.0 copy-start
  1.3 1.0 %copy-done = bf16[1,64,4096]{2,1,0:T(8,128)(2,1)S(1)} copy-done((bf16[1,64,4096]{2,1,0:T(8,128)(2,1)S(1)}, bf16[1,64,4096]{2,1,0:T(8,128)(2,1)}, u32[]{:S(2)}) %copy-start) | copy-done | bytes 524312
  2.4 0.0 copy-start.1
  2.4 0.9 %copy-done.1 = bf16[9,64,64]{2,1,0:T(8,128)(2,1)S(1)} copy-done((bf16[9,64,64]{2,1,0:T(8,128)(2,1)S(1)}, bf16[9,64,64]{2,1,0:T(8,128)(2,1)}, u32[]{:S(2)}) %copy-start.1) | copy-done | bytes 73752
  3.3 0.0 copy-start.2
  3.3 0.9 %copy-done.2 = bf16[9,64,64]{2,1,0:T(8,128)(2,1)S(1)} copy-done((bf16[9,64,64]{2,1,0:T(8,128)(2,1)S(1)}, bf16[9,64,64]{2,1,0:T(8,128)(2,1)}, u32[]{:S(2)}) %copy-start.2) | copy-done | bytes 73752
  4.2 0.0 copy-start.3
  4.2 0.9 %copy-done.3 = bf16[1,32,2048]{2,1,0:T(8,128)(2,1)S(1)} copy-done((bf16[1,32,2048]{2,1,0:T(8,128)(2,1)S(1)}, bf16[1,32,2048]{2,1,0:T(8,128)(2,1)}, u32[]{:S(2)}) %copy-start.3) | copy-done | bytes 131096
  5.1 66.0 %level.1 = (bf16[32,2048]{1,0:T(8,128)(2,1)S(1)}, bf16[64,4096]{1,0:T(8,128)(2,1)S(1)}, f32[9,64,64]{2,1,0:T(8,128)S(1)}, f32[9,64,64]{2,1,0:T(8,128)S(1)}) custom-call(bf16[64,4096]{1,0:T(8,128)(2,1)S(1)} %bitcast.4, bf16[9,64,64]{2,1,0:T(8,128)(2,1)S(1)} %copy-done.1, bf16[9,64,64]{2,1,0:T(8,128)(2,1)S(1)} %copy-done.2, bf16[32,2048]{1,0:T(8,128)(2,1)S(1)} %bitcast.7, ...), custom_call_target="tpu_custom_call" | custom-call | tf_op jit(solution)/shard_map/level/pallas_call | solution.py:573
  71.1 0.7 copy.15
  71.8 0.8 %copy.16 = bf16[1,64,4096]{2,1,0:T(8,128)(2,1)} copy(bf16[1,64,4096]{2,1,0:T(8,128)(2,1)S(1)} %bitcast.5) | data formatting | bytes 1048576
  72.6 0.7 copy.17
  73.3 0.7 copy.18
Async XLA Ops:
  0.6 0.7 copy-start.4
  0.6 0.7 copy-start.5
  0.7 0.7 copy-start.6
  1.3 1.0 %copy-start = (bf16[1,64,4096]{2,1,0:T(8,128)(2,1)S(1)}, bf16[1,64,4096]{2,1,0:T(8,128)(2,1)}, u32[]{:S(2)}) copy-start(bf16[1,64,4096]{2,1,0:T(8,128)(2,1)} %param.7) | copy-start | bytes 1572868
  2.4 0.9 %copy-start.1 = (bf16[9,64,64]{2,1,0:T(8,128)(2,1)S(1)}, bf16[9,64,64]{2,1,0:T(8,128)(2,1)}, u32[]{:S(2)}) copy-start(bf16[9,64,64]{2,1,0:T(8,128)(2,1)} %w1_ref.1) | copy-start | bytes 221188
  3.3 0.9 %copy-start.2 = (bf16[9,64,64]{2,1,0:T(8,128)(2,1)S(1)}, bf16[9,64,64]{2,1,0:T(8,128)(2,1)}, u32[]{:S(2)}) copy-start(bf16[9,64,64]{2,1,0:T(8,128)(2,1)} %w2_ref.1) | copy-start | bytes 221188
  4.2 0.9 %copy-start.3 = (bf16[1,32,2048]{2,1,0:T(8,128)(2,1)S(1)}, bf16[1,32,2048]{2,1,0:T(8,128)(2,1)}, u32[]{:S(2)}) copy-start(bf16[1,32,2048]{2,1,0:T(8,128)(2,1)} %param.10) | copy-start | bytes 393220

commit v2 on v1

v2 whole, which is shorter than its diff:
```python
import functools

import jax
import jax.numpy as jnp
from jax import lax
from jax.experimental import pallas as pl
from jax.experimental.pallas import tpu as pltpu
from jax.sharding import PartitionSpec as P

REACH = 3
SLOTS = 2 * REACH + 1
SIDE = 64
CHANS = 64
PAIRS = SIDE // 2
ROWS = PAIRS * SIDE
STRIP = 4 * SIDE
PLANE = 16
LEVELS = 8
SHARE = 9
CHUNK = 8
RIMS = 4 * SIDE + 32
MESH = pl.DeviceIdType.MESH
BF16 = jnp.bfloat16
F32 = jnp.float32
EDGE_DIRS = ((0, 2), (2, 1), (4, 0), (6, 3))
CORNER_DIRS = ((1, 2, False), (3, 0, False), (5, 0, True), (7, 2, True))
FAR_FIRST = (3, -3, 2, -2, 1, -1)
NEAR_FIRST = (1, -1, 2, -2, 3, -3)


def dot(a, b):
    return jnp.dot(a, b, preferred_element_type=F32)


def dot_rows(a, b):
    return lax.dot_general(a, b, (((0,), (0,)), ((), ())), preferred_element_type=F32)


def half_turn(x):
    return pltpu.roll(x, 64, axis=1)


def low_half(x):
    return lax.broadcasted_iota(jnp.int32, x.shape, 1) < 64


def swap(x, y):
    low = low_half(x)
    return jnp.where(low, x, half_turn(y)), jnp.where(low, half_turn(x), y)


def sigmoid(z):
    return 1.0 / (1.0 + jnp.exp(-z))


def plane_peer(here, member):
    return here // 32 * 32 + member * 2 + here % 2


def level_peer(here, member):
    return member * 32 + here % 32


def blocks_of(w_ref, dilation, turned):
    taps = [w_ref[t].astype(F32) for t in range(9)]
    if turned:
        taps = [jnp.transpose(tap) for tap in taps]
    zero = jnp.zeros((CHANS, CHANS), F32)
    result = {}
    for a in range(3):
        left, mid, right = taps[3 * a : 3 * a + 3]
        if dilation == 2:
            quads = {d: (w, zero, zero, w) for d, w in ((-1, left), (0, mid), (1, right))}
        else:
            quads = {-1: (zero, zero, left, zero), 0: (mid, left, right, mid), 1: (zero, right, zero, zero)}
        for d, (q00, q01, q10, q11) in quads.items():
            if turned:
                q01, q10 = q10, q01
                d = -d
            block = jnp.concatenate(
                [jnp.concatenate([q00, q01], 1), jnp.concatenate([q10, q11], 1)], 0
            )
            result[a, d] = block.astype(BF16)
    return result


def fill_weights(w_ref, dilation, turned, big):
    for (a, d), block in blocks_of(w_ref, dilation, turned).items():
        big[(d + 1) * 128 : (d + 2) * 128, a * 128 : (a + 1) * 128] = block


def combine(product, dilation, turned):
    rows = product.shape[0]
    up, mid, down = product[:, :128], product[:, 128:256], product[:, 256:]
    if turned:
        up, down = down, up
    i = lax.broadcasted_iota(jnp.int32, (rows, 128), 0) % SIDE
    up = jnp.where(i >= dilation, pltpu.roll(up, dilation, axis=0), 0.0)
    down = jnp.where(i < SIDE - dilation, pltpu.roll(down, rows - dilation, axis=0), 0.0)
    return mid + up + down


def neighbouring(x_ref, start, count):
    parts = [x_ref[pl.ds(start + k, count)].reshape(count * SIDE, 128) for k in range(3)]
    return jnp.concatenate(parts, 1)


def chunks(body):
    def step(c, unused):
        body(c)
        return unused

    lax.fori_loop(0, PAIRS // CHUNK, step, 0)


def chunk_rows(c):
    return pl.ds(pl.multiple_of(c * (CHUNK * SIDE), CHUNK * SIDE), CHUNK * SIDE)


def convolve(x_ref, big, z_ref, dilation):
    def body(c):
        product = dot(neighbouring(x_ref, c * CHUNK, CHUNK), big[...])
        z_ref[chunk_rows(c), :] = combine(product, dilation, False)

    chunks(body)


def keep_edges(edge_ref, c, value):
    value = value.reshape(CHUNK, SIDE, 128)
    place = pl.ds(pl.multiple_of(c * (CHUNK * 8), CHUNK * 8), CHUNK * 8)
    edge_ref[0, place, :] = value[:, :8].reshape(CHUNK * 8, 128)
    edge_ref[1, place, :] = value[:, SIDE - 8 :].reshape(CHUNK * 8, 128)


def edge_row(edge_ref, side, depth):
    return edge_ref[side, pl.ds(depth if side == 0 else 7 - depth, PAIRS, stride=8), :]


def write_strips(x_ref, edge_ref, strip_ref):
    top = swap(edge_row(edge_ref, 0, 0), edge_row(edge_ref, 0, 1))
    bottom = swap(edge_row(edge_ref, 1, 0), edge_row(edge_ref, 1, 1))
    strip_ref[0:64] = jnp.concatenate(top, 0).astype(BF16)
    strip_ref[64:128] = x_ref[1]
    strip_ref[128:192] = jnp.concatenate(bottom, 0).astype(BF16)
    strip_ref[192:256] = half_turn(x_ref[PAIRS].astype(F32)).astype(BF16)


def write_thin_strips(x_ref, edge_ref, strip_ref):
    strip_ref[0:64] = jnp.concatenate(swap(edge_row(edge_ref, 0, 0), edge_row(edge_ref, 1, 0)), 0).astype(BF16)
    first, last = x_ref[1].astype(F32), x_ref[PAIRS].astype(F32)
    strip_ref[64:128] = jnp.where(low_half(first), first, last).astype(BF16)


def fill_select(here, devices, nbr_ref, turn_ref, corner_ref, select, thin):
    def slot_of(j):
        return lax.rem(nbr_ref[0, j] - here + REACH + devices, devices)

    def columns_of(p, edge, quarter, flips):
        source = lax.rem(edge + 4 - quarter, 4)
        flip = jnp.where(quarter == flips[0], 1, jnp.where(quarter == flips[1], 1, 0))
        p = p + flip * (63 - 2 * p)
        split = (p % 2) * 32 + p // 2
        place = split + lax.rem(source, 2) * (p - split)
        return source * 64 + place, lax.rem(source, 2) * 64 + place

    lane = lax.broadcasted_iota(jnp.int32, (SIDE, STRIP), 1)
    row = lax.broadcasted_iota(jnp.int32, (SIDE, STRIP), 0)
    for n, (j, edge) in enumerate(EDGE_DIRS):
        if edge % 2 == 0:
            cols, thin_cols = columns_of(row % 32 * 2 + row // 32, edge, turn_ref[0, j], (2, 3))
        else:
            cols, thin_cols = columns_of(row, edge, turn_ref[0, j], (1, 2))
        hit = jnp.where(lane == cols, 1.0, 0.0)
        thin_hit = jnp.where(lane == thin_cols, 1.0, 0.0)[:, :128]
        slot = slot_of(j)
        for k in range(SLOTS):
            here_it_is = jnp.where(slot == k, 1.0, 0.0)
            select[k, n * 64 : (n + 1) * 64] = (hit * here_it_is).astype(BF16)
            thin[k, n * 64 : (n + 1) * 64] = (thin_hit * here_it_is).astype(BF16)
    lane = lane[:8]
    row = row[:8]
    hits = []
    for j, edge, last in CORNER_DIRS:
        cols, thin_cols = columns_of(63 - row if last else row, edge, turn_ref[0, j], (2, 3))
        keep = jnp.where(row < 2, 1.0, 0.0) * corner_ref[0, j // 2].astype(F32)
        hit = jnp.where(lane == cols, 1.0, 0.0) * keep
        thin_hit = (jnp.where(lane == thin_cols, 1.0, 0.0) * keep)[:, :128]
        hits.append((hit, thin_hit, slot_of(j)))
    for k in range(SLOTS):
        parts = [hit * jnp.where(slot == k, 1.0, 0.0) for hit, unused, slot in hits]
        select[k, 256:288] = jnp.concatenate(parts, 0).astype(BF16)
        parts = [hit * jnp.where(slot == k, 1.0, 0.0) for unused, hit, slot in hits]
        thin[k, 256:288] = jnp.concatenate(parts, 0).astype(BF16)


def exchange_halves(rims, turn_ref):
    parts = []
    places = [(j, edge, 64) for j, edge in EDGE_DIRS] + [(j, edge, 8) for j, edge, unused in CORNER_DIRS]
    start = 0
    for j, edge, count in places:
        block = rims[start : start + count]
        high = (lax.rem(edge + 4 - turn_ref[0, j], 4) // 2).astype(F32)
        parts.append(block * (1.0 - high) + half_turn(block) * high)
        start += count
    return jnp.concatenate(parts, 0)


def place_rims(rims, x_ref, rows_ref):
    north, east, south, west = (rims[64 * n : 64 * n + 64] for n in range(4))
    x_ref[PAIRS + 1] = east.astype(BF16)
    x_ref[0] = half_turn(west).astype(BF16)
    ne, se, sw, nw = (rims[256 + 8 * n : 264 + 8 * n] for n in range(4))
    for base, strip, right, left in ((0, north, ne, nw), (2, south, se, sw)):
        inner = swap(strip[:32], strip[32:])
        ends = swap(right[0:1], right[1:2])
        starts = swap(left[1:2], left[0:1])
        for d in range(2):
            rows_ref[base + d, 8:40, :] = inner[d]
            rows_ref[base + d, 40:41, :] = ends[d]
            rows_ref[base + d, 7:8, :] = starts[d]


def strips_beside(rows_ref):
    parts = []
    for k in range(4):
        parts.append(jnp.concatenate([rows_ref[k, 7 + d : 39 + d, :] for d in range(3)], 1))
    return jnp.concatenate(parts, 0).astype(BF16)


def add_rims(x_ref, beside, big, z_ref, dilation):
    west = combine(dot(x_ref[0], big[0:128, :]), dilation, False)
    z_ref[0:64, :] += west
    east = combine(dot(x_ref[PAIRS + 1], big[256:384, :]), dilation, False)
    z_ref[ROWS - 64 : ROWS, :] += east
    north = dot(beside[:64], big[:, 0:128])
    south = dot(beside[64:], big[:, 256:384])
    for d in range(dilation):
        z_ref[pl.ds(dilation - 1 - d, PAIRS, stride=SIDE), :] += north[32 * d : 32 * d + 32]
        z_ref[pl.ds(SIDE - dilation + d, PAIRS, stride=SIDE), :] += south[32 * d : 32 * d + 32]


def transposed(g_ref, big, z_ref, dilation):
    def body(c):
        product = dot(neighbouring(g_ref, c * CHUNK, CHUNK), big[...])
        z_ref[chunk_rows(c), :] = combine(product, dilation, True)

    chunks(body)


def leaving_rims(g_ref, edge_ref, rows_ref, big, dilation):
    before = combine(dot(g_ref[1], big[256:384, :]), dilation, True)
    after = combine(dot(g_ref[PAIRS], big[0:128, :]), dilation, True)
    strips, corners = [], []
    gap = jnp.zeros((6, 128), F32)
    for side in range(2):
        lines = []
        for d in range(2):
            if d < dilation:
                rows_ref[2 * side + d, 8:40, :] = edge_row(edge_ref, side, dilation - 1 - d)
                near = [rows_ref[2 * side + d, 6 + k : 46 + k, :] for k in range(3)]
                near = jnp.concatenate(near, 1).astype(BF16)
                lines.append(dot(near, big[:, 256 * side : 256 * side + 128]))
            else:
                lines.append(jnp.zeros((40, 128), F32))
        strips.append(jnp.concatenate(swap(lines[0][1:33], lines[1][1:33]), 0))
        first, second = swap(lines[0][33:34], lines[1][33:34])
        right = jnp.concatenate([first, second, gap], 0)
        second, first = swap(lines[0][0:1], lines[1][0:1])
        left = jnp.concatenate([first, second, gap], 0)
        corners.append((right, left))
    order = [strips[0], after, strips[1], half_turn(before)]
    order += [corners[0][0], corners[1][0], corners[1][1], corners[0][1]]
    return jnp.concatenate(order, 0)


def add_returned(strips, z_ref, dilation):
    z_ref[0:64, :] += strips[64:128]
    z_ref[ROWS - 64 : ROWS, :] += half_turn(strips[192:256])
    top = swap(strips[0:32], strips[32:64])
    bottom = swap(strips[128:160], strips[160:192])
    for d in range(dilation):
        z_ref[pl.ds(d, PAIRS, stride=SIDE), :] += top[d]
        z_ref[pl.ds(SIDE - 1 - d, PAIRS, stride=SIDE), :] += bottom[d]


def add_thin_returned(strips, z_ref):
    top, bottom = swap(strips[0:32], strips[32:64])
    z_ref[pl.ds(0, PAIRS, stride=SIDE), :] += top
    z_ref[pl.ds(SIDE - 1, PAIRS, stride=SIDE), :] += bottom
    sides = strips[64:128]
    low = low_half(sides)
    z_ref[0:64, :] += jnp.where(low, sides, 0.0)
    z_ref[ROWS - 64 : ROWS, :] += jnp.where(low, 0.0, sides)


def write_gradient(c, g, dilation, g_ref, shifted, edge_ref):
    rows = CHUNK * SIDE
    g_ref[pl.ds(c * CHUNK + 1, CHUNK)] = g.astype(BF16).reshape(CHUNK, SIDE, 128)
    i = lax.broadcasted_iota(jnp.int32, (rows, 128), 0) % SIDE
    up = jnp.where(i < SIDE - dilation, pltpu.roll(g, rows - dilation, axis=0), 0.0)
    down = jnp.where(i >= dilation, pltpu.roll(g, dilation, axis=0), 0.0)
    shifted[chunk_rows(c), 0:128] = up.astype(BF16)
    shifted[chunk_rows(c), 128:256] = g.astype(BF16)
    shifted[chunk_rows(c), 256:384] = down.astype(BF16)
    keep_edges(edge_ref, c, g)


def weight_gradient(x_ref, shifted, beside, edge_ref, raw, flat, dilation):
    strip_grads = []
    zero = jnp.zeros((PAIRS, 128), F32)
    for side in range(2):
        for d in range(2):
            if d >= dilation:
                part = jnp.zeros((PAIRS, 384), F32)
            else:
                row = edge_row(edge_ref, side, dilation - 1 - d)
                part = jnp.concatenate([row, zero, zero] if side == 0 else [zero, zero, row], 1)
            strip_grads.append(part)
    strip_grads = jnp.concatenate(strip_grads, 0).astype(BF16)
    for k in range(3):
        total = dot_rows(x_ref[k : k + PAIRS].reshape(ROWS, 128), shifted[...])
        raw[k] = total + dot_rows(beside[:, 128 * k : 128 * k + 128], strip_grads)
    taps = []
    for a in range(3):
        lanes = slice(128 * a, 128 * a + 128)
        upper = [raw[k, 0:64, lanes] for k in range(3)]
        lower = [raw[k, 64:128, lanes] for k in range(3)]
        if dilation == 2:
            taps += [upper[k] + half_turn(lower[k]) for k in range(3)]
        else:
            taps.append(half_turn(upper[1]) + lower[0])
            taps.append(upper[1] + half_turn(lower[1]))
            taps.append(lower[1] + half_turn(upper[2]))
    low = low_half(taps[0])
    for t in range(0, 8, 2):
        flat[32 * t : 32 * t + 64, :] = jnp.where(low, taps[t], half_turn(taps[t + 1]))
    flat[256:288, :] = jnp.where(low[:32], taps[8][:32], half_turn(taps[8][32:]))


def write_taps(total_ref, flat, out_ref):
    for n in range(2 * PLANE):
        flat[SHARE * n : SHARE * n + SHARE, :] = total_ref[n]
    for t in range(8):
        block = flat[t // 2 * 64 : t // 2 * 64 + 64, :]
        if t % 2 == 1:
            block = half_turn(block)
        out_ref[t] = block[:, :CHANS]
    last = flat[256:288, :]
    out_ref[8] = jnp.concatenate([last, half_turn(last)], 0)[:, :CHANS]


class Ring:
    def __init__(self, here, devices, source, target, send, recv):
        self.here, self.devices = here, devices
        self.source, self.target, self.send, self.recv = source, target, send, recv

    def copy(self, offset):
        return pltpu.make_async_remote_copy(
            src_ref=self.source(offset),
            dst_ref=self.target.at[REACH - offset],
            send_sem=self.send.at[REACH + offset],
            recv_sem=self.recv.at[REACH - offset],
            device_id=(lax.rem(self.here + offset + self.devices, self.devices),),
            device_id_type=MESH,
        )

    def start(self, offset):
        self.copy(offset).start()

    def arrived(self, slot):
        there = self.target.at[slot]
        pltpu.make_async_copy(there, there, self.recv.at[slot]).wait()

    def finish(self):
        for offset in FAR_FIRST:
            self.copy(offset).wait_send()


class Reduction:
    def __init__(self, here, src, other, half, plane, level, out, sems, core_sems):
        self.here, self.src, self.other, self.half = here, src, other, half
        self.plane, self.level, self.out = plane, level, out
        self.sems, self.core_sems = sems, core_sems
        self.core = here % 2
        self.me = here // 2 % PLANE
        self.floor = here // 32

    def core_copy(self, src, dst, step):
        return pltpu.make_async_remote_copy(
            src_ref=src, dst_ref=dst,
            send_sem=self.core_sems.at[step, 0], recv_sem=self.core_sems.at[step, 1],
            device_id=(self.here + 1 - 2 * self.core,), device_id_type=MESH,
        )

    def halving(self):
        return self.core_copy(self.src.at[pl.ds((1 - self.core) * PLANE, PLANE)], self.other, 0)

    def joining(self):
        mine = self.out.at[pl.ds(self.core * PLANE, PLANE)]
        return self.core_copy(mine, mine, 1)

    def scatter_copy(self, k):
        peer = (self.me + k) % PLANE
        return pltpu.make_async_remote_copy(
            src_ref=self.half.at[peer], dst_ref=self.plane.at[self.me],
            send_sem=self.sems.at[0, peer], recv_sem=self.sems.at[1, self.me],
            device_id=(plane_peer(self.here, peer),), device_id_type=MESH,
        )

    def level_copy(self, k):
        peer = (self.floor + k) % LEVELS
        return pltpu.make_async_remote_copy(
            src_ref=self.level.at[self.floor], dst_ref=self.level.at[self.floor],
            send_sem=self.sems.at[2, peer], recv_sem=self.sems.at[3, self.floor],
            device_id=(level_peer(self.here, peer),), device_id_type=MESH,
        )

    def gather_copy(self, k):
        peer = (self.me + k) % PLANE
        mine = self.out.at[self.core * PLANE + self.me]
        return pltpu.make_async_remote_copy(
            src_ref=mine, dst_ref=mine,
            send_sem=self.sems.at[4, peer], recv_sem=self.sems.at[5, self.me],
            device_id=(plane_peer(self.here, peer),), device_id_type=MESH,
        )

    def each(self, count, act):
        def body(k, unused):
            act(k)
            return unused

        lax.fori_loop(1, count, body, 0)

    def arrivals(self, count, buffer, row, mine, base):
        def one(k):
            peer = (mine + k) % count
            there = buffer.at[base + peer]
            pltpu.make_async_copy(there, there, self.sems.at[row, peer]).wait()

        self.each(count, one)

    def start(self, flat):
        for n in range(2 * PLANE):
            self.src[n] = flat[SHARE * n : SHARE * n + SHARE, :]
        self.halving().start()

    def scatter(self):
        self.halving().wait_recv()
        self.half[...] = self.src[pl.ds(self.core * PLANE, PLANE)] + self.other[...]
        self.each(PLANE, lambda k: self.scatter_copy(k).start())
        self.plane[self.me] = self.half[self.me]

    def across(self):
        self.arrivals(PLANE, self.plane, 1, self.me, 0)
        self.level[self.floor] = jnp.sum(self.plane[...], axis=0)
        self.each(LEVELS, lambda k: self.level_copy(k).start())

    def gather(self):
        self.arrivals(LEVELS, self.level, 3, self.floor, 0)
        self.out[self.core * PLANE + self.me] = jnp.sum(self.level[...], axis=0)
        self.each(PLANE, lambda k: self.gather_copy(k).start())

    def join(self):
        self.arrivals(PLANE, self.out, 5, self.me, self.core * PLANE)
        self.joining().start()

    def joined(self):
        theirs = self.out.at[pl.ds((1 - self.core) * PLANE, PLANE)]
        pltpu.make_async_copy(theirs, theirs, self.core_sems.at[1, 1]).wait()

    def sent(self):
        self.halving().wait_send()
        self.joining().wait_send()
        self.each(PLANE, lambda k: self.scatter_copy(k).wait_send())
        self.each(LEVELS, lambda k: self.level_copy(k).wait_send())
        self.each(PLANE, lambda k: self.gather_copy(k).wait_send())


def level_kernel(
    devices,
    f_hbm, w1_hbm, w2_hbm, cot_hbm, nbr_hbm, turn_hbm, corner_hbm,
    pooled_hbm, gin_hbm, dw1_hbm, dw2_hbm,
    f_ref, w1_ref, w2_ref, cot_ref, nbr_ref, turn_ref, corner_ref,
    pooled_ref, gin_ref, dw1_ref, dw2_ref,
    x1, x2, g_ref, shifted, z_ref, d_ref, act_ref, edge_ref, rows1, rows2, leave, raw, flat,
    big1, big1t, big2, big2t, select, thin,
    pool1, pool2, out2, back2, out1, back1,
    src2, other2, half2, plane2, level2, total2,
    src1, other1, half1, plane1, level1, total1,
    load_sems, store_sems, ring_sems, sems2, sems1, core_sems2, core_sems1,
):
    here = lax.axis_index("tiles")
    loads = (
        (f_hbm, f_ref), (nbr_hbm, nbr_ref), (turn_hbm, turn_ref), (corner_hbm, corner_ref),
        (w1_hbm, w1_ref), (w2_hbm, w2_ref), (cot_hbm, cot_ref),
    )
    loads = [pltpu.make_async_copy(a, b, load_sems.at[n]) for n, (a, b) in enumerate(loads)]
    for load in loads:
        load.start()
    stores = ((pooled_ref, pooled_hbm), (gin_ref, gin_hbm), (dw1_ref, dw1_hbm), (dw2_ref, dw2_hbm))
    stores = [pltpu.make_async_copy(a, b, store_sems.at[n]) for n, (a, b) in enumerate(stores)]
    barrier = pltpu.get_barrier_semaphore()

    def greet(device):
        pl.semaphore_signal(barrier, inc=1, device_id=(device,), device_id_type=MESH)

    for offset in FAR_FIRST:
        greet(lax.rem(here + offset + devices, devices))

    def greet_plane(k, unused):
        greet(plane_peer(here, (here // 2 + k) % PLANE))
        return unused

    def greet_level(k, unused):
        greet(level_peer(here, (here // 32 + k) % LEVELS))
        return unused

    lax.fori_loop(1, PLANE, greet_plane, 0)
    lax.fori_loop(1, LEVELS, greet_level, 0)

    ring1 = Ring(here, devices, lambda o: pool1.at[REACH], pool1, ring_sems.at[0], ring_sems.at[1])
    ring2 = Ring(here, devices, lambda o: pool2.at[REACH], pool2, ring_sems.at[2], ring_sems.at[3])
    ring3 = Ring(here, devices, lambda o: out2.at[REACH + o], back2, ring_sems.at[4], ring_sems.at[5])
    ring4 = Ring(here, devices, lambda o: out1.at[REACH + o], back1, ring_sems.at[6], ring_sems.at[7])
    sum2 = Reduction(here, src2, other2, half2, plane2, level2, total2, sems2, core_sems2)
    sum1 = Reduction(here, src1, other1, half1, plane1, level1, total1, sems1, core_sems1)

    def collect(ring, pool, chosen):
        rims = dot(chosen[REACH], pool[REACH])
        for offset in NEAR_FIRST:
            slot = REACH - offset
            ring.arrived(slot)
            rims = rims + dot(chosen[slot], pool[slot])
        return rims

    def send_back(ring, out_ref, rims, chosen):
        rims = rims.astype(BF16)
        for offset in FAR_FIRST:
            out_ref[REACH + offset] = dot_rows(chosen[REACH + offset], rims).astype(BF16)
            ring.start(offset)
        return dot_rows(chosen[REACH], rims)

    def take_back(ring, back_ref, own):
        for offset in NEAR_FIRST:
            ring.arrived(REACH - offset)
            own = own + back_ref[REACH - offset].astype(F32)
        return own

    empty = jnp.zeros((SIDE, 128), BF16)
    for x in (x1, x2, g_ref):
        x[0] = empty
        x[PAIRS + 1] = empty
    leave[...] = jnp.zeros_like(leave)
    loads[0].wait()
    for jp in range(PAIRS):
        x1[jp + 1] = f_ref[:, 128 * jp : 128 * jp + 128]
    for jp in range(PAIRS):
        edge_ref[0, 8 * jp : 8 * jp + 8, :] = f_ref[0:16, 128 * jp : 128 * jp + 128].astype(F32)[:8]
        edge_ref[1, 8 * jp : 8 * jp + 8, :] = f_ref[48:64, 128 * jp : 128 * jp + 128].astype(F32)[8:]
    write_thin_strips(x1, edge_ref, pool1.at[REACH])
    pl.semaphore_wait(barrier, 2 * REACH + PLANE - 1 + LEVELS - 1)
    for offset in FAR_FIRST:
        ring1.start(offset)

    for load in loads[1:]:
        load.wait()
    fill_weights(w1_ref, 1, False, big1)
    convolve(x1, big1, z_ref, 1)
    fill_select(here, devices, nbr_ref, turn_ref, corner_ref, select, thin)
    fill_weights(w2_ref, 2, False, big2)
    fill_weights(w2_ref, 2, True, big2t)
    fill_weights(w1_ref, 1, True, big1t)
    low = lax.broadcasted_iota(jnp.int32, (PAIRS, 128), 1) < 64
    for t in range(PAIRS // 2):
        both = cot_ref[:, 128 * t : 128 * t + 128].astype(F32) * 0.25
        turned = half_turn(both)
        for jp, value in ((2 * t, jnp.where(low, both, turned)), (2 * t + 1, jnp.where(low, turned, both))):
            act_ref[pl.ds(SIDE * jp, PAIRS, stride=2), :] = value
            act_ref[pl.ds(SIDE * jp + 1, PAIRS, stride=2), :] = value
    place_rims(exchange_halves(collect(ring1, pool1, thin), turn_ref), x1, rows1)
    beside1 = strips_beside(rows1)
    add_rims(x1, beside1, big1, z_ref, 1)

    def activate(c):
        z = z_ref[chunk_rows(c), :]
        s = sigmoid(z)
        y = z * s
        d_ref[chunk_rows(c), :] = s * (1.0 + z * (1.0 - s))
        x2[pl.ds(c * CHUNK + 1, CHUNK)] = y.astype(BF16).reshape(CHUNK, SIDE, 128)
        keep_edges(edge_ref, c, y)

    chunks(activate)
    write_strips(x2, edge_ref, pool2.at[REACH])
    for offset in FAR_FIRST:
        ring2.start(offset)

    convolve(x2, big2, z_ref, 2)
    place_rims(collect(ring2, pool2, select), x2, rows2)
    beside2 = strips_beside(rows2)
    add_rims(x2, beside2, big2, z_ref, 2)

    def second(c):
        z = z_ref[chunk_rows(c), :]
        s = sigmoid(z)
        z_ref[chunk_rows(c), :] = z * s * 0.25
        g = act_ref[chunk_rows(c), :] * s * (1.0 + z * (1.0 - s))
        write_gradient(c, g.astype(BF16).astype(F32), 2, g_ref, shifted, edge_ref)

    chunks(second)

    own = send_back(ring3, out2, leaving_rims(g_ref, edge_ref, leave, big2t, 2), select)
    weight_gradient(x2, shifted, beside2, edge_ref, raw, flat, 2)
    sum2.start(flat)
    for t in range(PAIRS // 2):
        sums = []
        for jp in (2 * t, 2 * t + 1):
            v = z_ref[pl.ds(SIDE * jp, PAIRS, stride=2), :] + z_ref[pl.ds(SIDE * jp + 1, PAIRS, stride=2), :]
            sums.append(v + half_turn(v))
        pooled_ref[:, 128 * t : 128 * t + 128] = jnp.where(low, sums[0], sums[1]).astype(BF16)
    stores[0].start()
    transposed(g_ref, big2t, z_ref, 2)
    sum2.scatter()
    add_returned(take_back(ring3, back2, own), z_ref, 2)

    def first(c):
        g = z_ref[chunk_rows(c), :] * d_ref[chunk_rows(c), :]
        write_gradient(c, g.astype(BF16).astype(F32), 1, g_ref, shifted, edge_ref)

    chunks(first)

    weight_gradient(x1, shifted, beside1, edge_ref, raw, flat, 1)
    sum1.start(flat)
    rims = exchange_halves(leaving_rims(g_ref, edge_ref, leave, big1t, 1), turn_ref)
    sum1.scatter()
    own = send_back(ring4, out1, rims, thin)
    sum2.across()
    transposed(g_ref, big1t, z_ref, 1)
    sum1.across()
    sum2.gather()
    add_thin_returned(take_back(ring4, back1, own), z_ref)
    for jp in range(PAIRS):
        gin_ref[:, 128 * jp : 128 * jp + 128] = z_ref[SIDE * jp : SIDE * jp + SIDE, :].astype(BF16)
    stores[1].start()
    sum1.gather()
    sum2.join()
    for ring in (ring1, ring2, ring3, ring4):
        ring.finish()
    sum2.joined()
    write_taps(total2, flat, dw2_ref)
    stores[3].start()
    sum2.sent()
    sum1.join()
    sum1.joined()
    write_taps(total1, flat, dw1_ref)
    stores[2].start()
    sum1.sent()
    for store in stores:
        store.wait()


def finish_kernel(*refs):
    ins, outs, held, (load_sems, store_sems) = refs[:4], refs[4:8], refs[8:12], refs[12:]
    loads = [pltpu.make_async_copy(ins[n], held[n], load_sems.at[n]) for n in range(4)]
    stores = [pltpu.make_async_copy(held[n], outs[n], store_sems.at[n]) for n in range(4)]
    for load in loads:
        load.start()
    for load, store in zip(loads, stores):
        load.wait()
        store.start()
    for store in stores:
        store.wait()


def local(features, weights_first, weights_second, cotangent, neighbours, turns, corners):
    devices = lax.axis_size("tiles")
    anywhere = pl.BlockSpec(memory_space=pl.ANY)
    inputs = (features[0], weights_first, weights_second, cotangent[0], neighbours, turns, corners)
    outputs = (
        jax.ShapeDtypeStruct((PAIRS, PAIRS * CHANS), BF16),
        jax.ShapeDtypeStruct((SIDE, SIDE * CHANS), BF16),
        jax.ShapeDtypeStruct((9, CHANS, CHANS), F32),
        jax.ShapeDtypeStruct((9, CHANS, CHANS), F32),
    )
    slabs = pltpu.VMEM((PAIRS + 2, SIDE, 128), BF16)
    field = pltpu.VMEM((ROWS, 128), F32)
    big = pltpu.VMEM((384, 384), BF16)
    pool = pltpu.VMEM((SLOTS, STRIP, 128), BF16)
    thin_pool = pltpu.VMEM((SLOTS, 128, 128), BF16)
    rows = pltpu.VMEM((4, 48, 128), F32)

    def shares(count):
        return pltpu.VMEM((count, SHARE, 128), F32)

    reduction = [shares(n) for n in (2 * PLANE, PLANE, PLANE, PLANE, LEVELS, 2 * PLANE)]
    results = pl.pallas_call(
        functools.partial(level_kernel, devices),
        out_shape=outputs,
        in_specs=[pl.BlockSpec(memory_space=pltpu.HBM)] * 7,
        out_specs=[anywhere] * 4,
        scratch_shapes=[pltpu.VMEM(x.shape, x.dtype) for x in inputs[:4]]
        + [pltpu.SMEM(x.shape, x.dtype) for x in inputs[4:]]
        + [pltpu.VMEM(x.shape, x.dtype) for x in outputs]
        + [
            slabs, slabs, slabs,
            pltpu.VMEM((ROWS, 384), BF16),
            field, field, field,
            pltpu.VMEM((2, 8 * PAIRS, 128), F32),
            rows, rows, rows,
            pltpu.VMEM((3, 128, 384), F32),
            pltpu.VMEM((2 * PLANE * SHARE, 128), F32),
            big, big, big, big,
            pltpu.VMEM((SLOTS, RIMS, STRIP), BF16),
            pltpu.VMEM((SLOTS, RIMS, 128), BF16),
            thin_pool, pool, pool, pool, thin_pool, thin_pool,
        ]
        + reduction
        + reduction
        + [
            pltpu.SemaphoreType.DMA((7,)),
            pltpu.SemaphoreType.DMA((4,)),
            pltpu.SemaphoreType.DMA((8, SLOTS)),
            pltpu.SemaphoreType.DMA((6, PLANE)),
            pltpu.SemaphoreType.DMA((6, PLANE)),
            pltpu.SemaphoreType.DMA((2, 2)),
            pltpu.SemaphoreType.DMA((2, 2)),
        ],
        compiler_params=pltpu.CompilerParams(
            collective_id=0, has_side_effects=True, vmem_limit_bytes=60 * 2**20
        ),
        name="level",
    )(*inputs)
    pooled, grad, first, second = pl.pallas_call(
        finish_kernel,
        out_shape=outputs,
        in_specs=[anywhere] * 4,
        out_specs=[anywhere] * 4,
        scratch_shapes=[pltpu.VMEM(x.shape, x.dtype) for x in outputs]
        + [pltpu.SemaphoreType.DMA((4,))] * 2,
        compiler_params=pltpu.CompilerParams(vmem_limit_bytes=60 * 2**20),
        name="finish",
    )(*results)
    return pooled[None], grad[None], first, second


def solution(mesh):
    return jax.shard_map(
        local,
        mesh=mesh,
        in_specs=(
            P("tiles", None, None),
            P(),
            P(),
            P("tiles", None, None),
            P("tiles", None),
            P("tiles", None),
            P("tiles", None),
        ),
        out_specs=(P("tiles", None, None), P("tiles", None, None), P(), P()),
        check_vma=False,
    )
```

time: 74.2 us -> 61.7 us (0.83)
  local copies, waits for them, and re-layouts: 7.3 us -> 0 us
  Pallas kernels: 66 us -> 60.9 us
    unnamed x18 -> x0, local copies, waits for them, and re-layouts: 7.3 us -> none
    pallas_call x1 -> x2, Pallas kernels: 66 us -> 60.9 us  [the longest x1 58.7 us: local(): pl.pallas_call(functools.partial(level_kernel, devices), out_shape=output...]
where the time goes in v2:
time: 61.7 us; the launch traced here: 61.5 us
  Pallas kernels  60.9 us (99%)
  between operations  0.64 us (1%)
    pallas_call x1, Pallas kernels, local(): pl.pallas_call(functools.partial(level_kernel, devices), out_shape=output...  58.7 us
    pallas_call x1, Pallas kernels, local(): pl.pallas_call(finish_kernel, out_shape=outputs, in_specs=[anywhere] * 4,...  2.17 us

profile of v2, /device:TPU:1, one launch (start us, length us, event | category | flops | bytes accessed | tf_op | source)
XLA Modules:
  0.0 61.5 jit_solution(8949077696751224235)
XLA Ops:
  0.6 58.7 %level.1 = (bf16[32,2048]{1,0:T(8,128)(2,1)}, bf16[64,4096]{1,0:T(8,128)(2,1)}, f32[9,64,64]{2,1,0:T(8,128)}, f32[9,64,64]{2,1,0:T(8,128)}) custom-call(bf16[64,4096]{1,0:T(8,128)(2,1)} %bitcast.4, bf16[9,64,64]{2,1,0:T(8,128)(2,1)} %w1_hbm.1, bf16[9,64,64]{2,1,0:T(8,128)(2,1)} %w2_hbm.1, bf16[32,2048]{1,0:T(8,128)(2,1)} %bitcast.5, s32[1,8]{1,0:T(1,128)} %nbr_hbm.1, ...), custom_call_target="tpu_custom_call" | custom-call | tf_op jit(solution)/shard_map/level/pallas_call | solution.py:695
  59.4 2.2 %finish.1 = (bf16[32,2048]{1,0:T(8,128)(2,1)}, bf16[64,4096]{1,0:T(8,128)(2,1)}, f32[9,64,64]{2,1,0:T(8,128)}, f32[9,64,64]{2,1,0:T(8,128)}) custom-call(bf16[32,2048]{1,0:T(8,128)(2,1)} %get-tuple-element.12.refs_0_, bf16[64,4096]{1,0:T(8,128)(2,1)} %get-tuple-element.13.refs_1_, f32[9,64,64]{2,1,0:T(8,128)} %get-tuple-element.14.refs_2_, ...), custom_call_target="tpu_custom_call" | custom-call | tf_op jit(solution)/shard_map/finish/pallas_call | solution.py:732

commit v3 on v2

v3 whole, which is shorter than its diff:
```python
import functools

import jax
import jax.numpy as jnp
from jax import lax
from jax.experimental import pallas as pl
from jax.experimental.pallas import tpu as pltpu
from jax.sharding import PartitionSpec as P

REACH = 3
SLOTS = 2 * REACH + 1
SIDE = 64
CHANS = 64
PAIRS = SIDE // 2
ROWS = PAIRS * SIDE
STRIP = 4 * SIDE
PLANE = 32
LEVELS = 8
SHARE = 9
CHUNK = 8
RIMS = 4 * SIDE + 32
MESH = pl.DeviceIdType.MESH
BF16 = jnp.bfloat16
F32 = jnp.float32
EDGE_DIRS = ((0, 2), (2, 1), (4, 0), (6, 3))
CORNER_DIRS = ((1, 2, False), (3, 0, False), (5, 0, True), (7, 2, True))
OFFSETS = (1, -1, 2, -2, 3, -3)


def dot(a, b):
    return jnp.dot(a, b, preferred_element_type=F32)


def dot_rows(a, b):
    return lax.dot_general(a, b, (((0,), (0,)), ((), ())), preferred_element_type=F32)


def half_turn(x):
    return pltpu.roll(x, 64, axis=1)


def low_half(x):
    return lax.broadcasted_iota(jnp.int32, x.shape, 1) < 64


def swap(x, y):
    low = low_half(x)
    return jnp.where(low, x, half_turn(y)), jnp.where(low, half_turn(x), y)


def sigmoid(z):
    return 1.0 / (1.0 + jnp.exp(-z))


def hops(steps, size):
    return min(steps, size - steps)


PLANE_STEPS = sorted(
    ((x, y, core) for x in range(4) for y in range(4) for core in range(2) if x or y or core),
    key=lambda step: -(hops(step[0], 4) + hops(step[1], 4)),
)
LEVEL_STEPS = sorted(range(1, LEVELS), key=lambda step: -hops(step, LEVELS))


def plane_members(here):
    x, y, core = here // 8 % 4, here // 2 % 4, here % 2
    xs = [8 * ((x + step) % 4) for step in range(4)]
    ys = [2 * ((y + step) % 4) for step in range(4)]
    cores = [core, 1 - core]
    return [xs[a] + ys[b] + cores[c] for a, b, c in PLANE_STEPS]


def level_members(here):
    return [(here // PLANE + step) % LEVELS for step in LEVEL_STEPS]


def blocks_of(w_ref, dilation, turned):
    taps = [w_ref[t].astype(F32) for t in range(9)]
    if turned:
        taps = [jnp.transpose(tap) for tap in taps]
    zero = jnp.zeros((CHANS, CHANS), F32)
    result = {}
    for a in range(3):
        left, mid, right = taps[3 * a : 3 * a + 3]
        if dilation == 2:
            quads = {d: (w, zero, zero, w) for d, w in ((-1, left), (0, mid), (1, right))}
        else:
            quads = {-1: (zero, zero, left, zero), 0: (mid, left, right, mid), 1: (zero, right, zero, zero)}
        for d, (q00, q01, q10, q11) in quads.items():
            if turned:
                q01, q10 = q10, q01
                d = -d
            block = jnp.concatenate(
                [jnp.concatenate([q00, q01], 1), jnp.concatenate([q10, q11], 1)], 0
            )
            result[a, d] = block.astype(BF16)
    return result


def fill_weights(w_ref, dilation, turned, big):
    for (a, d), block in blocks_of(w_ref, dilation, turned).items():
        big[(d + 1) * 128 : (d + 2) * 128, a * 128 : (a + 1) * 128] = block


def combine(product, dilation, turned):
    rows = product.shape[0]
    up, mid, down = product[:, :128], product[:, 128:256], product[:, 256:]
    if turned:
        up, down = down, up
    i = lax.broadcasted_iota(jnp.int32, (rows, 128), 0) % SIDE
    up = jnp.where(i >= dilation, pltpu.roll(up, dilation, axis=0), 0.0)
    down = jnp.where(i < SIDE - dilation, pltpu.roll(down, rows - dilation, axis=0), 0.0)
    return mid + up + down


def neighbouring(x_ref, start, count):
    parts = [x_ref[pl.ds(start + k, count)].reshape(count * SIDE, 128) for k in range(3)]
    return jnp.concatenate(parts, 1)


def chunks(body):
    def step(c, unused):
        body(c)
        return unused

    lax.fori_loop(0, PAIRS // CHUNK, step, 0)


def chunk_rows(c):
    return pl.ds(pl.multiple_of(c * (CHUNK * SIDE), CHUNK * SIDE), CHUNK * SIDE)


def convolve(x_ref, big, z_ref, dilation):
    def body(c):
        product = dot(neighbouring(x_ref, c * CHUNK, CHUNK), big[...])
        z_ref[chunk_rows(c), :] = combine(product, dilation, False)

    chunks(body)


def edge_row(edge_ref, side, depth):
    return edge_ref[side, pl.ds(depth if side == 0 else 7 - depth, PAIRS, stride=8), :]


def border_of(make):
    rows = {}
    for depth in range(2):
        rows[0, depth] = make(pl.ds(depth, PAIRS, stride=SIDE))
        rows[1, depth] = make(pl.ds(SIDE - 1 - depth, PAIRS, stride=SIDE))
    return rows, make(slice(0, SIDE)), make(slice(ROWS - SIDE, ROWS))


def write_strips(border, strip_ref):
    rows, first, last = border
    strip_ref[0:64] = jnp.concatenate(swap(rows[0, 0], rows[0, 1]), 0).astype(BF16)
    strip_ref[64:128] = first.astype(BF16)
    strip_ref[128:192] = jnp.concatenate(swap(rows[1, 0], rows[1, 1]), 0).astype(BF16)
    strip_ref[192:256] = half_turn(last).astype(BF16)


def write_thin_strips(x_ref, edge_ref, strip_ref):
    strip_ref[0:64] = jnp.concatenate(swap(edge_row(edge_ref, 0, 0), edge_row(edge_ref, 1, 0)), 0).astype(BF16)
    first, last = x_ref[1].astype(F32), x_ref[PAIRS].astype(F32)
    strip_ref[64:128] = jnp.where(low_half(first), first, last).astype(BF16)


def fill_select(here, devices, nbr_ref, turn_ref, corner_ref, select, thin):
    def slot_of(j):
        return lax.rem(nbr_ref[0, j] - here + REACH + devices, devices)

    def columns_of(p, edge, quarter, flips):
        source = lax.rem(edge + 4 - quarter, 4)
        flip = jnp.where(quarter == flips[0], 1, jnp.where(quarter == flips[1], 1, 0))
        p = p + flip * (63 - 2 * p)
        split = (p % 2) * 32 + p // 2
        place = split + lax.rem(source, 2) * (p - split)
        return source * 64 + place, lax.rem(source, 2) * 64 + place

    lane = lax.broadcasted_iota(jnp.int32, (SIDE, STRIP), 1)
    row = lax.broadcasted_iota(jnp.int32, (SIDE, STRIP), 0)
    for n, (j, edge) in enumerate(EDGE_DIRS):
        if edge % 2 == 0:
            cols, thin_cols = columns_of(row % 32 * 2 + row // 32, edge, turn_ref[0, j], (2, 3))
        else:
            cols, thin_cols = columns_of(row, edge, turn_ref[0, j], (1, 2))
        hit = jnp.where(lane == cols, 1.0, 0.0)
        thin_hit = jnp.where(lane == thin_cols, 1.0, 0.0)[:, :128]
        slot = slot_of(j)
        for k in range(SLOTS):
            here_it_is = jnp.where(slot == k, 1.0, 0.0)
            select[k, n * 64 : (n + 1) * 64] = (hit * here_it_is).astype(BF16)
            thin[k, n * 64 : (n + 1) * 64] = (thin_hit * here_it_is).astype(BF16)
    lane = lane[:8]
    row = row[:8]
    hits = []
    for j, edge, last in CORNER_DIRS:
        cols, thin_cols = columns_of(63 - row if last else row, edge, turn_ref[0, j], (2, 3))
        keep = jnp.where(row < 2, 1.0, 0.0) * corner_ref[0, j // 2].astype(F32)
        hit = jnp.where(lane == cols, 1.0, 0.0) * keep
        thin_hit = (jnp.where(lane == thin_cols, 1.0, 0.0) * keep)[:, :128]
        hits.append((hit, thin_hit, slot_of(j)))
    for k in range(SLOTS):
        parts = [hit * jnp.where(slot == k, 1.0, 0.0) for hit, unused, slot in hits]
        select[k, 256:288] = jnp.concatenate(parts, 0).astype(BF16)
        parts = [hit * jnp.where(slot == k, 1.0, 0.0) for unused, hit, slot in hits]
        thin[k, 256:288] = jnp.concatenate(parts, 0).astype(BF16)


def exchange_halves(rims, turn_ref):
    parts = []
    places = [(j, edge, 64) for j, edge in EDGE_DIRS] + [(j, edge, 8) for j, edge, unused in CORNER_DIRS]
    start = 0
    for j, edge, count in places:
        block = rims[start : start + count]
        high = (lax.rem(edge + 4 - turn_ref[0, j], 4) // 2).astype(F32)
        parts.append(block * (1.0 - high) + half_turn(block) * high)
        start += count
    return jnp.concatenate(parts, 0)


def place_rims(rims, x_ref, rows_ref):
    north, east, south, west = (rims[64 * n : 64 * n + 64] for n in range(4))
    x_ref[PAIRS + 1] = east.astype(BF16)
    x_ref[0] = half_turn(west).astype(BF16)
    ne, se, sw, nw = (rims[256 + 8 * n : 264 + 8 * n] for n in range(4))
    for base, strip, right, left in ((0, north, ne, nw), (2, south, se, sw)):
        inner = swap(strip[:32], strip[32:])
        ends = swap(right[0:1], right[1:2])
        starts = swap(left[1:2], left[0:1])
        for d in range(2):
            rows_ref[base + d, 8:40, :] = inner[d]
            rows_ref[base + d, 40:41, :] = ends[d]
            rows_ref[base + d, 7:8, :] = starts[d]


def keep_outer_rows(edge_ref, outer):
    for depth in range(3):
        outer[1 + depth, 8:40, :] = edge_row(edge_ref, 0, depth)
        outer[6 - depth, 8:40, :] = edge_row(edge_ref, 1, depth)


def finish_outer_rows(x_ref, rows_ref, outer, beside):
    outer[0] = rows_ref[0]
    outer[7] = rows_ref[2]
    for place, x in ((7, x_ref[0].astype(F32)), (40, x_ref[PAIRS + 1].astype(F32))):
        for n in range(3):
            outer[1 + n, place : place + 1, :] = x[n : n + 1]
            outer[4 + n, place : place + 1, :] = x[SIDE - 3 + n : SIDE - 2 + n]
    for n in range(8):
        beside[n] = jnp.concatenate([outer[n, 7 + d : 39 + d, :] for d in range(3)], 1).astype(BF16)


def strips_beside(rows_ref):
    parts = []
    for k in range(4):
        parts.append(jnp.concatenate([rows_ref[k, 7 + d : 39 + d, :] for d in range(3)], 1))
    return jnp.concatenate(parts, 0).astype(BF16)


def add_rims(x_ref, beside, big, z_ref, dilation):
    west = combine(dot(x_ref[0], big[0:128, :]), dilation, False)
    z_ref[0:64, :] += west
    east = combine(dot(x_ref[PAIRS + 1], big[256:384, :]), dilation, False)
    z_ref[ROWS - 64 : ROWS, :] += east
    north = dot(beside[:64], big[:, 0:128])
    south = dot(beside[64:], big[:, 256:384])
    for d in range(dilation):
        z_ref[pl.ds(dilation - 1 - d, PAIRS, stride=SIDE), :] += north[32 * d : 32 * d + 32]
        z_ref[pl.ds(SIDE - dilation + d, PAIRS, stride=SIDE), :] += south[32 * d : 32 * d + 32]


def transposed(g_ref, big, z_ref, dilation):
    def body(c):
        product = dot(neighbouring(g_ref, c * CHUNK, CHUNK), big[...])
        z_ref[chunk_rows(c), :] = combine(product, dilation, True)

    chunks(body)


def leaving_rims(border, rows_ref, big, dilation):
    rows, first, last = border
    before = combine(dot(first.astype(BF16), big[256:384, :]), dilation, True)
    after = combine(dot(last.astype(BF16), big[0:128, :]), dilation, True)
    strips, corners = [], []
    gap = jnp.zeros((6, 128), F32)
    for side in range(2):
        lines = []
        for d in range(2):
            if d < dilation:
                rows_ref[2 * side + d, 8:40, :] = rows[side, dilation - 1 - d]
                near = [rows_ref[2 * side + d, 6 + k : 46 + k, :] for k in range(3)]
                near = jnp.concatenate(near, 1).astype(BF16)
                lines.append(dot(near, big[:, 256 * side : 256 * side + 128]))
            else:
                lines.append(jnp.zeros((40, 128), F32))
        strips.append(jnp.concatenate(swap(lines[0][1:33], lines[1][1:33]), 0))
        upper, lower = swap(lines[0][33:34], lines[1][33:34])
        right = jnp.concatenate([upper, lower, gap], 0)
        lower, upper = swap(lines[0][0:1], lines[1][0:1])
        left = jnp.concatenate([upper, lower, gap], 0)
        corners.append((right, left))
    order = [strips[0], after, strips[1], half_turn(before)]
    order += [corners[0][0], corners[1][0], corners[1][1], corners[0][1]]
    return jnp.concatenate(order, 0)


def add_returned(strips, z_ref, dilation):
    z_ref[0:64, :] += strips[64:128]
    z_ref[ROWS - 64 : ROWS, :] += half_turn(strips[192:256])
    top = swap(strips[0:32], strips[32:64])
    bottom = swap(strips[128:160], strips[160:192])
    for d in range(dilation):
        z_ref[pl.ds(d, PAIRS, stride=SIDE), :] += top[d]
        z_ref[pl.ds(SIDE - 1 - d, PAIRS, stride=SIDE), :] += bottom[d]


def add_thin_returned(strips, z_ref):
    top, bottom = swap(strips[0:32], strips[32:64])
    z_ref[pl.ds(0, PAIRS, stride=SIDE), :] += top
    z_ref[pl.ds(SIDE - 1, PAIRS, stride=SIDE), :] += bottom
    sides = strips[64:128]
    low = low_half(sides)
    z_ref[0:64, :] += jnp.where(low, sides, 0.0)
    z_ref[ROWS - 64 : ROWS, :] += jnp.where(low, 0.0, sides)


def row_shifts(g, dilation):
    rows = g.shape[0]
    i = lax.broadcasted_iota(jnp.int32, g.shape, 0) % SIDE
    up = jnp.where(i < SIDE - dilation, pltpu.roll(g, rows - dilation, axis=0), 0.0)
    down = jnp.where(i >= dilation, pltpu.roll(g, dilation, axis=0), 0.0)
    return up.astype(BF16), g.astype(BF16), down.astype(BF16)


def store_shifts(c, g, dilation, shifted):
    for n, moved in enumerate(row_shifts(g, dilation)):
        shifted[chunk_rows(c), 128 * n : 128 * n + 128] = moved


def store_slabs(c, g, g_ref):
    g_ref[pl.ds(c * CHUNK + 1, CHUNK)] = g.astype(BF16).reshape(CHUNK, SIDE, 128)


def inner_products(x_ref, shifted, raw):
    for k in range(3):
        raw[k] = dot_rows(x_ref[k : k + PAIRS].reshape(ROWS, 128), shifted[...])


def strip_products(beside, border, raw):
    rows = border[0]
    zero = jnp.zeros((PAIRS, 128), F32)
    grads = [jnp.concatenate([rows[0, 1 - d], zero, zero], 1) for d in range(2)]
    grads += [jnp.concatenate([zero, zero, rows[1, 1 - d]], 1) for d in range(2)]
    grads = jnp.concatenate(grads, 0).astype(BF16)
    for k in range(3):
        raw[k] += dot_rows(beside[:, 128 * k : 128 * k + 128], grads)


def without_outer_rows(g):
    i = lax.broadcasted_iota(jnp.int32, g.shape, 0) % SIDE
    return jnp.where(i < 2, 0.0, jnp.where(i >= SIDE - 2, 0.0, g))


def border_products(x_ref, outer, border, raw):
    rows, first, last = border
    grads = jnp.concatenate([rows[0, 0], rows[0, 1], rows[1, 1], rows[1, 0]], 0).astype(BF16)
    by_row = []
    for a in range(3):
        near = jnp.concatenate([outer[n] for n in (a, a + 1, a + 4, a + 5)], 0)
        by_row.append(dot_rows(near, grads))
    by_row = jnp.concatenate(by_row, 1)
    left = jnp.concatenate(row_shifts(without_outer_rows(first), 1), 1)
    right = jnp.concatenate(row_shifts(without_outer_rows(last), 1), 1)
    sides = jnp.concatenate([left, right], 0)
    for k in range(3):
        near = jnp.concatenate([x_ref[k], x_ref[PAIRS - 1 + k]], 0)
        raw[k] += by_row[128 * k : 128 * k + 128] + dot_rows(near, sides)


def pack_taps(raw, flat, dilation):
    taps = []
    for a in range(3):
        lanes = slice(128 * a, 128 * a + 128)
        upper = [raw[k, 0:64, lanes] for k in range(3)]
        lower = [raw[k, 64:128, lanes] for k in range(3)]
        if dilation == 2:
            taps += [upper[k] + half_turn(lower[k]) for k in range(3)]
        else:
            taps.append(half_turn(upper[1]) + lower[0])
            taps.append(upper[1] + half_turn(lower[1]))
            taps.append(lower[1] + half_turn(upper[2]))
    low = low_half(taps[0])
    for t in range(0, 8, 2):
        flat[32 * t : 32 * t + 64, :] = jnp.where(low, taps[t], half_turn(taps[t + 1]))
    flat[256:288, :] = jnp.where(low[:32], taps[8][:32], half_turn(taps[8][32:]))


def write_taps(total_ref, flat, out_ref):
    for n in range(PLANE):
        flat[SHARE * n : SHARE * n + SHARE, :] = total_ref[n]
    for t in range(8):
        block = flat[t // 2 * 64 : t // 2 * 64 + 64, :]
        if t % 2 == 1:
            block = half_turn(block)
        out_ref[t] = block[:, :CHANS]
    last = flat[256:288, :]
    out_ref[8] = jnp.concatenate([last, half_turn(last)], 0)[:, :CHANS]


class Ring:
    def __init__(self, peers, source, target, send, recv):
        self.peers, self.source, self.target, self.send, self.recv = peers, source, target, send, recv

    def copy(self, offset):
        return pltpu.make_async_remote_copy(
            src_ref=self.source(offset),
            dst_ref=self.target.at[REACH - offset],
            send_sem=self.send.at[REACH + offset],
            recv_sem=self.recv.at[REACH - offset],
            device_id=(self.peers[offset],),
            device_id_type=MESH,
        )

    def start(self, offset):
        self.copy(offset).start()

    def arrived(self, slot):
        there = self.target.at[slot]
        pltpu.make_async_copy(there, there, self.recv.at[slot]).wait()

    def finish(self):
        for offset in OFFSETS:
            self.copy(offset).wait_send()


class Reduction:
    def __init__(self, here, members, levels, src, plane, level, out, sems):
        self.src, self.plane, self.level, self.out, self.sems = src, plane, level, out, sems
        self.me = here % PLANE
        self.floor = here // PLANE
        self.members = members
        self.in_plane = [here - self.me + member for member in members]
        self.levels = levels
        self.in_column = [PLANE * floor + self.me for floor in levels]

    def copies(self, step):
        result = []
        for n, device in enumerate(self.in_column if step == 1 else self.in_plane):
            if step == 0:
                src, dst = self.src.at[self.members[n]], self.plane.at[n]
            elif step == 1:
                src = dst = self.level.at[self.floor]
            else:
                src = dst = self.out.at[self.me]
            result.append(
                pltpu.make_async_remote_copy(
                    src_ref=src, dst_ref=dst,
                    send_sem=self.sems.at[2 * step, n], recv_sem=self.sems.at[2 * step + 1, n],
                    device_id=(device,), device_id_type=MESH,
                )
            )
        return result

    def start(self, step):
        for copy in self.copies(step):
            copy.start()

    def arrived(self, step):
        for n in range(len(self.levels if step == 1 else self.members)):
            there = (self.plane.at[n], self.level.at[self.levels[n % 7]], self.out.at[self.members[n]])[step]
            pltpu.make_async_copy(there, there, self.sems.at[2 * step + 1, n]).wait()

    def sent(self, step):
        for copy in self.copies(step):
            copy.wait_send()

    def scatter(self, flat):
        for n in range(PLANE):
            self.src[n] = flat[SHARE * n : SHARE * n + SHARE, :]
        self.start(0)
        self.plane[PLANE - 1] = self.src[self.me]

    def across(self):
        self.arrived(0)
        self.level[self.floor] = jnp.sum(self.plane[...], axis=0)
        self.start(1)

    def gather(self):
        self.arrived(1)
        self.out[self.me] = jnp.sum(self.level[...], axis=0)
        self.start(2)

    def gathered(self):
        for step in range(3):
            self.sent(step)
        self.arrived(2)


def level_kernel(
    devices,
    f_hbm, w1_hbm, w2_hbm, cot_hbm, nbr_hbm, turn_hbm, corner_hbm,
    pooled_hbm, gin_hbm, dw1_hbm, dw2_hbm,
    f_ref, w1_ref, w2_ref, cot_ref, nbr_ref, turn_ref, corner_ref,
    pooled_ref, gin_ref, dw1_ref, dw2_ref,
    x1, x2, g_ref, shifted, z_ref, d_ref, act_ref, edge_ref, rows1, rows2, leave, outer, near_outer, raw, flat,
    big1, big1t, big2, big2t, select, select_turned, thin,
    pool1, pool2, out2, back2, out1, back1,
    src2, plane2, level2, total2,
    src1, plane1, level1, total1,
    load_sems, store_sems, ring_sems, sems2, sems1,
):
    here = lax.axis_index("tiles")
    loads = (
        (f_hbm, f_ref), (nbr_hbm, nbr_ref), (turn_hbm, turn_ref), (corner_hbm, corner_ref),
        (w1_hbm, w1_ref), (w2_hbm, w2_ref), (cot_hbm, cot_ref),
    )
    loads = [pltpu.make_async_copy(a, b, load_sems.at[n]) for n, (a, b) in enumerate(loads)]
    for load in loads:
        load.start()
    stores = ((pooled_ref, pooled_hbm), (gin_ref, gin_hbm), (dw1_ref, dw1_hbm), (dw2_ref, dw2_hbm))
    stores = [pltpu.make_async_copy(a, b, store_sems.at[n]) for n, (a, b) in enumerate(stores)]
    barrier = pltpu.get_barrier_semaphore()

    peers = {offset: lax.rem(here + offset + devices, devices) for offset in OFFSETS}
    members, levels = plane_members(here), level_members(here)
    floor = here // PLANE * PLANE
    greeted = [PLANE * level + here % PLANE for level in levels]
    greeted += [floor + member for member in members]
    greeted += [peers[offset] for offset in OFFSETS]
    for device in greeted:
        pl.semaphore_signal(barrier, inc=1, device_id=(device,), device_id_type=MESH)

    ring1 = Ring(peers, lambda o: pool1.at[REACH], pool1, ring_sems.at[0], ring_sems.at[1])
    ring2 = Ring(peers, lambda o: pool2.at[REACH], pool2, ring_sems.at[2], ring_sems.at[3])
    ring3 = Ring(peers, lambda o: out2.at[REACH + o], back2, ring_sems.at[4], ring_sems.at[5])
    ring4 = Ring(peers, lambda o: out1.at[REACH + o], back1, ring_sems.at[6], ring_sems.at[7])
    sum2 = Reduction(here, members, levels, src2, plane2, level2, total2, sems2)
    sum1 = Reduction(here, members, levels, src1, plane1, level1, total1, sems1)

    def collect(ring, pool, chosen):
        rims = dot(chosen[REACH], pool[REACH])
        for offset in OFFSETS:
            slot = REACH - offset
            ring.arrived(slot)
            rims = rims + dot(chosen[slot], pool[slot])
        return rims

    def send_back(ring, out_ref, rims, product):
        rims = rims.astype(BF16)
        for offset in OFFSETS:
            out_ref[REACH + offset] = product(REACH + offset, rims).astype(BF16)
            ring.start(offset)
        return product(REACH, rims)

    def take_back(ring, back_ref, own):
        for offset in OFFSETS:
            ring.arrived(REACH - offset)
            own = own + back_ref[REACH - offset].astype(F32)
        return own

    empty = jnp.zeros((SIDE, 128), BF16)
    for x in (x1, x2, g_ref):
        x[0] = empty
        x[PAIRS + 1] = empty
    leave[...] = jnp.zeros_like(leave)
    loads[0].wait()
    for jp in range(PAIRS):
        x1[jp + 1] = f_ref[:, 128 * jp : 128 * jp + 128]
    for jp in range(PAIRS):
        edge_ref[0, 8 * jp : 8 * jp + 8, :] = f_ref[0:16, 128 * jp : 128 * jp + 128].astype(F32)[:8]
        edge_ref[1, 8 * jp : 8 * jp + 8, :] = f_ref[48:64, 128 * jp : 128 * jp + 128].astype(F32)[8:]
    write_thin_strips(x1, edge_ref, pool1.at[REACH])
    pl.semaphore_wait(barrier, len(greeted))
    for offset in OFFSETS:
        ring1.start(offset)

    for load in loads[1:]:
        load.wait()
    fill_weights(w1_ref, 1, False, big1)
    convolve(x1, big1, z_ref, 1)
    fill_select(here, devices, nbr_ref, turn_ref, corner_ref, select, thin)
    fill_weights(w2_ref, 2, False, big2)
    fill_weights(w2_ref, 2, True, big2t)
    fill_weights(w1_ref, 1, True, big1t)
    low = lax.broadcasted_iota(jnp.int32, (PAIRS, 128), 1) < 64
    for t in range(PAIRS // 2):
        both = cot_ref[:, 128 * t : 128 * t + 128].astype(F32) * 0.25
        turned = half_turn(both)
        for jp, value in ((2 * t, jnp.where(low, both, turned)), (2 * t + 1, jnp.where(low, turned, both))):
            act_ref[pl.ds(SIDE * jp, PAIRS, stride=2), :] = value
            act_ref[pl.ds(SIDE * jp + 1, PAIRS, stride=2), :] = value
    keep_outer_rows(edge_ref, outer)
    for k in range(SLOTS):
        select_turned[k] = jnp.transpose(select[k].astype(F32)).astype(BF16)
    place_rims(exchange_halves(collect(ring1, pool1, thin), turn_ref), x1, rows1)
    add_rims(x1, strips_beside(rows1), big1, z_ref, 1)

    def outer_y(place):
        z = z_ref[place, :]
        return z * sigmoid(z)

    write_strips(border_of(outer_y), pool2.at[REACH])
    for offset in OFFSETS:
        ring2.start(offset)

    def activate(c):
        z = z_ref[chunk_rows(c), :]
        s = sigmoid(z)
        y = z * s
        d_ref[chunk_rows(c), :] = s * (1.0 + z * (1.0 - s))
        store_slabs(c, y, x2)

    chunks(activate)
    finish_outer_rows(x1, rows1, outer, near_outer)

    convolve(x2, big2, z_ref, 2)
    place_rims(collect(ring2, pool2, select), x2, rows2)
    beside2 = strips_beside(rows2)
    add_rims(x2, beside2, big2, z_ref, 2)

    def second_gradient(place):
        z = z_ref[place, :]
        s = sigmoid(z)
        g = act_ref[place, :] * s * (1.0 + z * (1.0 - s))
        return g.astype(BF16).astype(F32)

    border2 = border_of(second_gradient)
    rims = leaving_rims(border2, leave, big2t, 2)
    own = send_back(ring3, out2, rims, lambda k, x: dot(select_turned[k], x))

    def second(c):
        z = z_ref[chunk_rows(c), :]
        s = sigmoid(z)
        z_ref[chunk_rows(c), :] = z * s * 0.25
        g = (act_ref[chunk_rows(c), :] * s * (1.0 + z * (1.0 - s))).astype(BF16).astype(F32)
        store_slabs(c, g, g_ref)
        store_shifts(c, g, 2, shifted)

    chunks(second)
    inner_products(x2, shifted, raw)
    strip_products(beside2, border2, raw)
    pack_taps(raw, flat, 2)
    sum2.scatter(flat)
    for t in range(PAIRS // 2):
        sums = []
        for jp in (2 * t, 2 * t + 1):
            v = z_ref[pl.ds(SIDE * jp, PAIRS, stride=2), :] + z_ref[pl.ds(SIDE * jp + 1, PAIRS, stride=2), :]
            sums.append(v + half_turn(v))
        pooled_ref[:, 128 * t : 128 * t + 128] = jnp.where(low, sums[0], sums[1]).astype(BF16)
    stores[0].start()
    transposed(g_ref, big2t, z_ref, 2)

    def inside(c):
        g = without_outer_rows(z_ref[chunk_rows(c), :] * d_ref[chunk_rows(c), :])
        store_shifts(c, g, 1, shifted)

    chunks(inside)
    shifted[0:SIDE] = jnp.zeros((SIDE, 384), BF16)
    shifted[ROWS - SIDE : ROWS] = jnp.zeros((SIDE, 384), BF16)
    inner_products(x1, shifted, raw)
    sum2.across()
    add_returned(take_back(ring3, back2, own), z_ref, 2)

    def first_gradient(place):
        return (z_ref[place, :] * d_ref[place, :]).astype(BF16).astype(F32)

    border1 = border_of(first_gradient)
    border_products(x1, near_outer, border1, raw)
    pack_taps(raw, flat, 1)
    sum1.scatter(flat)
    rims = exchange_halves(leaving_rims(border1, leave, big1t, 1), turn_ref)
    own = send_back(ring4, out1, rims, lambda k, x: dot_rows(thin[k], x))

    def first(c):
        store_slabs(c, z_ref[chunk_rows(c), :] * d_ref[chunk_rows(c), :], g_ref)

    chunks(first)
    sum2.gather()
    transposed(g_ref, big1t, z_ref, 1)
    sum1.across()
    add_thin_returned(take_back(ring4, back1, own), z_ref)
    for jp in range(PAIRS):
        gin_ref[:, 128 * jp : 128 * jp + 128] = z_ref[SIDE * jp : SIDE * jp + SIDE, :].astype(BF16)
    stores[1].start()
    sum1.gather()
    sum2.gathered()
    for ring in (ring1, ring2, ring3, ring4):
        ring.finish()
    write_taps(total2, flat, dw2_ref)
    stores[3].start()
    sum1.gathered()
    write_taps(total1, flat, dw1_ref)
    stores[2].start()
    for store in stores:
        store.wait()


def finish_kernel(*refs):
    copies = [pltpu.make_async_copy(refs[n], refs[4 + n], refs[8].at[n]) for n in range(4)]
    for copy in copies:
        copy.start()
    for copy in copies:
        copy.wait()


def local(features, weights_first, weights_second, cotangent, neighbours, turns, corners):
    devices = lax.axis_size("tiles")
    anywhere = pl.BlockSpec(memory_space=pl.ANY)
    inputs = (features[0], weights_first, weights_second, cotangent[0], neighbours, turns, corners)
    inputs = tuple(pltpu.with_memory_space_constraint(x, pltpu.HBM) for x in inputs)
    outputs = (
        jax.ShapeDtypeStruct((PAIRS, PAIRS * CHANS), BF16),
        jax.ShapeDtypeStruct((SIDE, SIDE * CHANS), BF16),
        jax.ShapeDtypeStruct((9, CHANS, CHANS), F32),
        jax.ShapeDtypeStruct((9, CHANS, CHANS), F32),
    )
    slabs = pltpu.VMEM((PAIRS + 2, SIDE, 128), BF16)
    field = pltpu.VMEM((ROWS, 128), F32)
    big = pltpu.VMEM((384, 384), BF16)
    pool = pltpu.VMEM((SLOTS, STRIP, 128), BF16)
    thin_pool = pltpu.VMEM((SLOTS, 128, 128), BF16)
    rows = pltpu.VMEM((4, 48, 128), F32)

    def shares(count):
        return pltpu.VMEM((count, SHARE, 128), F32)

    reduction = [shares(n) for n in (PLANE, PLANE, LEVELS, PLANE)]
    results = pl.pallas_call(
        functools.partial(level_kernel, devices),
        out_shape=tuple(pltpu.VMEM(x.shape, x.dtype) for x in outputs),
        in_specs=[pl.BlockSpec(memory_space=pltpu.HBM)] * 7,
        out_specs=[anywhere] * 4,
        scratch_shapes=[pltpu.VMEM(x.shape, x.dtype) for x in inputs[:4]]
        + [pltpu.SMEM(x.shape, x.dtype) for x in inputs[4:]]
        + [pltpu.VMEM(x.shape, x.dtype) for x in outputs]
        + [
            slabs, slabs, slabs,
            pltpu.VMEM((ROWS, 384), BF16),
            field, field, field,
            pltpu.VMEM((2, 8 * PAIRS, 128), F32),
            rows, rows, rows,
            pltpu.VMEM((8, 48, 128), F32),
            pltpu.VMEM((8, PAIRS, 384), BF16),
            pltpu.VMEM((3, 128, 384), F32),
            pltpu.VMEM((2 * PLANE * SHARE, 128), F32),
            big, big, big, big,
            pltpu.VMEM((SLOTS, RIMS, STRIP), BF16),
            pltpu.VMEM((SLOTS, STRIP, RIMS), BF16),
            pltpu.VMEM((SLOTS, RIMS, 128), BF16),
            thin_pool, pool, pool, pool, thin_pool, thin_pool,
        ]
        + reduction
        + reduction
        + [
            pltpu.SemaphoreType.DMA((7,)),
            pltpu.SemaphoreType.DMA((4,)),
            pltpu.SemaphoreType.DMA((8, SLOTS)),
            pltpu.SemaphoreType.DMA((6, PLANE)),
            pltpu.SemaphoreType.DMA((6, PLANE)),
        ],
        compiler_params=pltpu.CompilerParams(
            collective_id=0, has_side_effects=True, vmem_limit_bytes=48 * 2**20
        ),
        name="level",
    )(*inputs)
    pooled, grad, first, second = pl.pallas_call(
        finish_kernel,
        out_shape=outputs,
        in_specs=[anywhere] * 4,
        out_specs=[anywhere] * 4,
        scratch_shapes=[pltpu.SemaphoreType.DMA((4,))],
        compiler_params=pltpu.CompilerParams(vmem_limit_bytes=4 * 2**20),
        name="finish",
    )(*results)
    return pooled[None], grad[None], first, second


def solution(mesh):
    return jax.shard_map(
        local,
        mesh=mesh,
        in_specs=(
            P("tiles", None, None),
            P(),
            P(),
            P("tiles", None, None),
            P("tiles", None),
            P("tiles", None),
            P("tiles", None),
        ),
        out_specs=(P("tiles", None, None), P("tiles", None, None), P(), P()),
        check_vma=False,
    )
```

time: 61.7 us -> 59.3 us (0.961)
  Pallas kernels: 60.9 us -> 58.5 us
    pallas_call x1, Pallas kernels: 58.7 us -> 57.4 us  [local(): pl.pallas_call(functools.partial(level_kernel, devices), out_shape=tuple(...]
    pallas_call x1, Pallas kernels: 2.17 us -> 1.06 us  [local(): pl.pallas_call(finish_kernel, out_shape=outputs, in_specs=[anywhere] * 4,...]
where the time goes in v3:
time: 59.3 us; the launch traced here: 59.1 us
  Pallas kernels  58.5 us (99%)
  between operations  0.64 us (1%)
    pallas_call x1, Pallas kernels, local(): pl.pallas_call(functools.partial(level_kernel, devices), out_shape=tuple(...  57.4 us

profile of v3, /device:TPU:1, one launch (start us, length us, event | category | flops | bytes accessed | tf_op | source)
XLA Modules:
  0.0 59.1 jit_solution(11191798367012145497)
XLA Ops:
  0.6 57.4 %level.1 = (bf16[32,2048]{1,0:T(8,128)(2,1)S(1)}, bf16[64,4096]{1,0:T(8,128)(2,1)S(1)}, f32[9,64,64]{2,1,0:T(8,128)S(1)}, f32[9,64,64]{2,1,0:T(8,128)S(1)}) custom-call(bf16[64,4096]{1,0:T(8,128)(2,1)} %bitcast.4, bf16[9,64,64]{2,1,0:T(8,128)(2,1)} %w1_hbm.1, bf16[9,64,64]{2,1,0:T(8,128)(2,1)} %w2_hbm.1, bf16[32,2048]{1,0:T(8,128)(2,1)} %bitcast.5, ...), custom_call_target="tpu_custom_call" | custom-call | tf_op jit(solution)/shard_map/level/pallas_call | solution.py:729
  58.1 1.1 %finish.1 = (bf16[32,2048]{1,0:T(8,128)(2,1)}, bf16[64,4096]{1,0:T(8,128)(2,1)}, f32[9,64,64]{2,1,0:T(8,128)}, f32[9,64,64]{2,1,0:T(8,128)}) custom-call(bf16[32,2048]{1,0:T(8,128)(2,1)S(1)} %get-tuple-element.12.refs_0_, bf16[64,4096]{1,0:T(8,128)(2,1)S(1)} %get-tuple-element.13.refs_1_, f32[9,64,64]{2,1,0:T(8,128)S(1)} %get-tuple-element.14.refs_2_, ...), custom_call_target="tpu_custom_call" | custom-call | tf_op jit(solution)/shard_map/finish/pallas_call | solution.py:767

commit v4 on v3

--- a/solution.py
+++ b/solution.py
@@ -467,8 +467,12 @@
             copy.start()
 
     def arrived(self, step):
-        for n in range(len(self.levels if step == 1 else self.members)):
-            there = (self.plane.at[n], self.level.at[self.levels[n % 7]], self.out.at[self.members[n]])[step]
+        places = (
+            [self.plane.at[n] for n in range(len(self.members))],
+            [self.level.at[n] for n in self.levels],
+            [self.out.at[n] for n in self.members],
+        )
+        for n, there in enumerate(places[step]):
             pltpu.make_async_copy(there, there, self.sems.at[2 * step + 1, n]).wait()
 
     def sent(self, step):
@@ -500,15 +504,14 @@
 def level_kernel(
     devices,
     f_hbm, w1_hbm, w2_hbm, cot_hbm, nbr_hbm, turn_hbm, corner_hbm,
-    pooled_hbm, gin_hbm, dw1_hbm, dw2_hbm,
+    pooled_ref, gin_ref, dw1_ref, dw2_ref,
     f_ref, w1_ref, w2_ref, cot_ref, nbr_ref, turn_ref, corner_ref,
-    pooled_ref, gin_ref, dw1_ref, dw2_ref,
     x1, x2, g_ref, shifted, z_ref, d_ref, act_ref, edge_ref, rows1, rows2, leave, outer, near_outer, raw, flat,
     big1, big1t, big2, big2t, select, select_turned, thin,
     pool1, pool2, out2, back2, out1, back1,
     src2, plane2, level2, total2,
     src1, plane1, level1, total1,
-    load_sems, store_sems, ring_sems, sems2, sems1,
+    load_sems, ring_sems, sems2, sems1,
 ):
     here = lax.axis_index("tiles")
     loads = (
@@ -518,8 +521,6 @@
     loads = [pltpu.make_async_copy(a, b, load_sems.at[n]) for n, (a, b) in enumerate(loads)]
     for load in loads:
         load.start()
-    stores = ((pooled_ref, pooled_hbm), (gin_ref, gin_hbm), (dw1_ref, dw1_hbm), (dw2_ref, dw2_hbm))
-    stores = [pltpu.make_async_copy(a, b, store_sems.at[n]) for n, (a, b) in enumerate(stores)]
     barrier = pltpu.get_barrier_semaphore()
 
     peers = {offset: lax.rem(here + offset + devices, devices) for offset in OFFSETS}
@@ -641,14 +642,12 @@
     inner_products(x2, shifted, raw)
     strip_products(beside2, border2, raw)
     pack_taps(raw, flat, 2)
-    sum2.scatter(flat)
     for t in range(PAIRS // 2):
         sums = []
         for jp in (2 * t, 2 * t + 1):
             v = z_ref[pl.ds(SIDE * jp, PAIRS, stride=2), :] + z_ref[pl.ds(SIDE * jp + 1, PAIRS, stride=2), :]
             sums.append(v + half_turn(v))
         pooled_ref[:, 128 * t : 128 * t + 128] = jnp.where(low, sums[0], sums[1]).astype(BF16)
-    stores[0].start()
     transposed(g_ref, big2t, z_ref, 2)
 
     def inside(c):
@@ -659,7 +658,7 @@
     shifted[0:SIDE] = jnp.zeros((SIDE, 384), BF16)
     shifted[ROWS - SIDE : ROWS] = jnp.zeros((SIDE, 384), BF16)
     inner_products(x1, shifted, raw)
-    sum2.across()
+    sum2.scatter(flat)
     add_returned(take_back(ring3, back2, own), z_ref, 2)
 
     def first_gradient(place):
@@ -670,30 +669,26 @@
     pack_taps(raw, flat, 1)
     sum1.scatter(flat)
     rims = exchange_halves(leaving_rims(border1, leave, big1t, 1), turn_ref)
-    own = send_back(ring4, out1, rims, lambda k, x: dot_rows(thin[k], x))
 
     def first(c):
         store_slabs(c, z_ref[chunk_rows(c), :] * d_ref[chunk_rows(c), :], g_ref)
 
     chunks(first)
+    transposed(g_ref, big1t, z_ref, 1)
+    sum2.across()
+    sum1.across()
+    own = send_back(ring4, out1, rims, lambda k, x: dot_rows(thin[k], x))
     sum2.gather()
-    transposed(g_ref, big1t, z_ref, 1)
-    sum1.across()
+    sum1.gather()
     add_thin_returned(take_back(ring4, back1, own), z_ref)
     for jp in range(PAIRS):
         gin_ref[:, 128 * jp : 128 * jp + 128] = z_ref[SIDE * jp : SIDE * jp + SIDE, :].astype(BF16)
-    stores[1].start()
-    sum1.gather()
     sum2.gathered()
     for ring in (ring1, ring2, ring3, ring4):
         ring.finish()
     write_taps(total2, flat, dw2_ref)
-    stores[3].start()
     sum1.gathered()
     write_taps(total1, flat, dw1_ref)
-    stores[2].start()
-    for store in stores:
-        store.wait()
 
 
 def finish_kernel(*refs):
@@ -730,10 +725,9 @@
         functools.partial(level_kernel, devices),
         out_shape=tuple(pltpu.VMEM(x.shape, x.dtype) for x in outputs),
         in_specs=[pl.BlockSpec(memory_space=pltpu.HBM)] * 7,
-        out_specs=[anywhere] * 4,
+        out_specs=[pl.BlockSpec(memory_space=pltpu.VMEM)] * 4,
         scratch_shapes=[pltpu.VMEM(x.shape, x.dtype) for x in inputs[:4]]
         + [pltpu.SMEM(x.shape, x.dtype) for x in inputs[4:]]
-        + [pltpu.VMEM(x.shape, x.dtype) for x in outputs]
         + [
             slabs, slabs, slabs,
             pltpu.VMEM((ROWS, 384), BF16),
@@ -754,7 +748,6 @@
         + reduction
         + [
             pltpu.SemaphoreType.DMA((7,)),
-            pltpu.SemaphoreType.DMA((4,)),
             pltpu.SemaphoreType.DMA((8, SLOTS)),
             pltpu.SemaphoreType.DMA((6, PLANE)),
             pltpu.SemaphoreType.DMA((6, PLANE)),

time: 59.3 us -> 57.8 us (0.975)
  Pallas kernels: 58.5 us -> 57.1 us
    pallas_call x1, Pallas kernels: 57.4 us -> 56 us  [local(): pl.pallas_call(functools.partial(level_kernel, devices), out_shape=tuple(...]
where the time goes in v4:
time: 57.8 us; the launch traced here: 57.7 us
  Pallas kernels  57.1 us (99%)
  between operations  0.64 us (1%)
    pallas_call x1, Pallas kernels, local(): pl.pallas_call(functools.partial(level_kernel, devices), out_shape=tuple(...  56 us

profile of v4, /device:TPU:1, one launch (start us, length us, event | category | flops | bytes accessed | tf_op | source)
XLA Modules:
  0.0 57.7 jit_solution(5732992153344447315)
XLA Ops:
  0.6 56.0 %level.1 = (bf16[32,2048]{1,0:T(8,128)(2,1)S(1)}, bf16[64,4096]{1,0:T(8,128)(2,1)S(1)}, f32[9,64,64]{2,1,0:T(8,128)S(1)}, f32[9,64,64]{2,1,0:T(8,128)S(1)}) custom-call(bf16[64,4096]{1,0:T(8,128)(2,1)} %bitcast.4, bf16[9,64,64]{2,1,0:T(8,128)(2,1)} %w1_hbm.1, bf16[9,64,64]{2,1,0:T(8,128)(2,1)} %w2_hbm.1, bf16[32,2048]{1,0:T(8,128)(2,1)} %bitcast.5, ...), custom_call_target="tpu_custom_call" | custom-call | tf_op jit(solution)/shard_map/level/pallas_call | solution.py:724
  56.7 1.1 %finish.1 = (bf16[32,2048]{1,0:T(8,128)(2,1)}, bf16[64,4096]{1,0:T(8,128)(2,1)}, f32[9,64,64]{2,1,0:T(8,128)}, f32[9,64,64]{2,1,0:T(8,128)}) custom-call(bf16[32,2048]{1,0:T(8,128)(2,1)S(1)} %get-tuple-element.12.refs_0_, bf16[64,4096]{1,0:T(8,128)(2,1)S(1)} %get-tuple-element.13.refs_1_, f32[9,64,64]{2,1,0:T(8,128)S(1)} %get-tuple-element.14.refs_2_, ...), custom_call_target="tpu_custom_call" | custom-call | tf_op jit(solution)/shard_map/finish/pallas_call | solution.py:760

commit v5 on v4

--- a/solution.py
+++ b/solution.py
@@ -472,7 +472,7 @@
             [self.level.at[n] for n in self.levels],
             [self.out.at[n] for n in self.members],
         )
-        for n, there in enumerate(places[step]):
+        for n, there in reversed(list(enumerate(places[step]))):
             pltpu.make_async_copy(there, there, self.sems.at[2 * step + 1, n]).wait()
 
     def sent(self, step):
@@ -526,9 +526,9 @@
     peers = {offset: lax.rem(here + offset + devices, devices) for offset in OFFSETS}
     members, levels = plane_members(here), level_members(here)
     floor = here // PLANE * PLANE
-    greeted = [PLANE * level + here % PLANE for level in levels]
+    greeted = [peers[offset] for offset in OFFSETS]
+    greeted += [PLANE * level + here % PLANE for level in levels]
     greeted += [floor + member for member in members]
-    greeted += [peers[offset] for offset in OFFSETS]
     for device in greeted:
         pl.semaphore_signal(barrier, inc=1, device_id=(device,), device_id_type=MESH)
 

time: 57.8 us -> 57.3 us (level)
  no operation moved by 1% of the time
where the time goes in v5:
time: 57.3 us; the launch traced here: 57.2 us
  Pallas kernels  56.6 us (99%)
  between operations  0.64 us (1%)
    pallas_call x1, Pallas kernels, local(): pl.pallas_call(functools.partial(level_kernel, devices), out_shape=tuple(...  55.5 us

profile of v5, /device:TPU:1, one launch (start us, length us, event | category | flops | bytes accessed | tf_op | source)
XLA Modules:
  0.0 57.2 jit_solution(16467423764714898571)
XLA Ops:
  0.6 55.5 %level.1 = (bf16[32,2048]{1,0:T(8,128)(2,1)S(1)}, bf16[64,4096]{1,0:T(8,128)(2,1)S(1)}, f32[9,64,64]{2,1,0:T(8,128)S(1)}, f32[9,64,64]{2,1,0:T(8,128)S(1)}) custom-call(bf16[64,4096]{1,0:T(8,128)(2,1)} %bitcast.4, bf16[9,64,64]{2,1,0:T(8,128)(2,1)} %w1_hbm.1, bf16[9,64,64]{2,1,0:T(8,128)(2,1)} %w2_hbm.1, bf16[32,2048]{1,0:T(8,128)(2,1)} %bitcast.5, ...), custom_call_target="tpu_custom_call" | custom-call | tf_op jit(solution)/shard_map/level/pallas_call | solution.py:724
  56.2 1.1 %finish.1 = (bf16[32,2048]{1,0:T(8,128)(2,1)}, bf16[64,4096]{1,0:T(8,128)(2,1)}, f32[9,64,64]{2,1,0:T(8,128)}, f32[9,64,64]{2,1,0:T(8,128)}) custom-call(bf16[32,2048]{1,0:T(8,128)(2,1)S(1)} %get-tuple-element.12.refs_0_, bf16[64,4096]{1,0:T(8,128)(2,1)S(1)} %get-tuple-element.13.refs_1_, f32[9,64,64]{2,1,0:T(8,128)S(1)} %get-tuple-element.14.refs_2_, ...), custom_call_target="tpu_custom_call" | custom-call | tf_op jit(solution)/shard_map/finish/pallas_call | solution.py:760

commit v6 on v5

--- a/solution.py
+++ b/solution.py
@@ -566,7 +566,7 @@
         x[PAIRS + 1] = empty
     leave[...] = jnp.zeros_like(leave)
     loads[0].wait()
-    for jp in range(PAIRS):
+    for jp in (0, PAIRS - 1):
         x1[jp + 1] = f_ref[:, 128 * jp : 128 * jp + 128]
     for jp in range(PAIRS):
         edge_ref[0, 8 * jp : 8 * jp + 8, :] = f_ref[0:16, 128 * jp : 128 * jp + 128].astype(F32)[:8]
@@ -575,6 +575,8 @@
     pl.semaphore_wait(barrier, len(greeted))
     for offset in OFFSETS:
         ring1.start(offset)
+    for jp in range(1, PAIRS - 1):
+        x1[jp + 1] = f_ref[:, 128 * jp : 128 * jp + 128]
 
     for load in loads[1:]:
         load.wait()

time: 57.3 us -> 57.3 us (level)
  no operation moved by 1% of the time
where the time goes in v6:
time: 57.3 us; the launch traced here: 57.2 us
  Pallas kernels  56.6 us (99%)
  between operations  0.64 us (1%)
    pallas_call x1, Pallas kernels, local(): pl.pallas_call(functools.partial(level_kernel, devices), out_shape=tuple(...  55.5 us

profile of v6, /device:TPU:1, one launch (start us, length us, event | category | flops | bytes accessed | tf_op | source)
XLA Modules:
  0.0 57.2 jit_solution(2764123185589252485)
XLA Ops:
  0.6 55.5 %level.1 = (bf16[32,2048]{1,0:T(8,128)(2,1)S(1)}, bf16[64,4096]{1,0:T(8,128)(2,1)S(1)}, f32[9,64,64]{2,1,0:T(8,128)S(1)}, f32[9,64,64]{2,1,0:T(8,128)S(1)}) custom-call(bf16[64,4096]{1,0:T(8,128)(2,1)} %bitcast.4, bf16[9,64,64]{2,1,0:T(8,128)(2,1)} %w1_hbm.1, bf16[9,64,64]{2,1,0:T(8,128)(2,1)} %w2_hbm.1, bf16[32,2048]{1,0:T(8,128)(2,1)} %bitcast.5, ...), custom_call_target="tpu_custom_call" | custom-call | tf_op jit(solution)/shard_map/level/pallas_call | solution.py:726
  56.2 1.1 %finish.1 = (bf16[32,2048]{1,0:T(8,128)(2,1)}, bf16[64,4096]{1,0:T(8,128)(2,1)}, f32[9,64,64]{2,1,0:T(8,128)}, f32[9,64,64]{2,1,0:T(8,128)}) custom-call(bf16[32,2048]{1,0:T(8,128)(2,1)S(1)} %get-tuple-element.12.refs_0_, bf16[64,4096]{1,0:T(8,128)(2,1)S(1)} %get-tuple-element.13.refs_1_, f32[9,64,64]{2,1,0:T(8,128)S(1)} %get-tuple-element.14.refs_2_, ...), custom_call_target="tpu_custom_call" | custom-call | tf_op jit(solution)/shard_map/finish/pallas_call | solution.py:762
